TPU v7x, 32 devices: a whole 2x2x4 slice. The times are simulated.
32 devices in a mesh: gal: 8 (over z, y), qry: 4 (over x, core).
Axes of the slice: x: 2, y: 2, z: 4, core: 2. Of those that a mesh axis runs over, the one named last changes fastest.
Arguments:
- descriptors: bfloat16 [16384, 512], P('gal'), may hold values from -6 to 6
- query_descriptors: bfloat16 [512, 512], P('qry'), may hold values from -6 to 6
- tile_blocks: int32 [512, 2], P('gal'), may hold values from 0 to 127, as said below
- neighbours: int32 [512, 12, 128], P('gal'), may hold values from 0 to 127
Outputs:
- ranking: float32 [16384, 512], P('gal', 'qry')
- residual: float32 [16384, 512], P('gal', 'qry')
Inputs may be any that keep to these rules, and one draw needn't show every extreme that they name: `tile_blocks`: every tile of the rows of one index of gal (tiles i * 64 to (i + 1) * 64 - 1 for index i) has its block row among that index's blocks i * 16 .. (i + 1) * 16 - 1, and its block column among the blocks of that index and of the two indices beside it, (i - 1) * 16 to (i + 2) * 16 - 1 within 0 to 127. A tile may be listed twice.
All inputs are finite; a program needn't handle non-finite values.
Results may differ from a plain program's by a relative error of at most 0.0003.
Values may be sent and summed in bfloat16 or wider, within the bound.
A program may use at most 128 MiB of HBM per device.

v0:
```python
import math

import jax
import jax.numpy as jnp
from jax import lax
from jax.sharding import PartitionSpec as P

D = 512
BLK = 128
KT = 12
ITERS = 3


damping = 0.99


def from_behind(value, axis, steps):
    count = lax.axis_size(axis)
    leading, last = (max(0, -steps), min(count, count - steps))
    return lax.ppermute(value, axis, [(source, source + steps) for source in range(leading, last)])


def padded(array, sides, width):
    for axis, dim in sides:
        devices, length = (lax.axis_size(axis), array.shape[dim])
        up = [(i, (i + 1) % devices) for i in range(devices - 1)]
        down = [(j, i) for i, j in up]
        last = lax.slice_in_dim(array, length - width, length, axis=dim)
        leading = lax.slice_in_dim(array, 0, width, axis=dim)
        before = lax.ppermute(last, axis, up)
        after = lax.ppermute(leading, axis, down)
        array = jnp.concatenate([before, array, after], axis=dim)
    return array


def build_tiles(window_blocks, row_place, col_place, neighbours):
    left = window_blocks[row_place]
    right = window_blocks[col_place]
    dots = jnp.einsum("tid,tjd->tij", left, right, preferred_element_type=jnp.float32)
    positions = jnp.arange(BLK, dtype=jnp.int32)
    counted = jnp.zeros(dots.shape, jnp.float32)
    for entry in range(KT):
        counted = counted + (neighbours[:, entry, :, None] == positions[None, None, :]).astype(
            jnp.float32
        )
    return counted * jax.nn.softplus(dots / math.sqrt(D))


def send_back(spread, rows_dev):
    below = spread[:rows_dev]
    middle = spread[rows_dev : 2 * rows_dev]
    above = spread[2 * rows_dev :]
    from_above = from_behind(below, "gal", -1)
    from_below = from_behind(above, "gal", 1)
    return middle + from_above + from_below


def column_squares(current):
    return lax.psum(jnp.sum(current * current, axis=0), "gal")


def per_device(descriptors, query_descriptors, tile_blocks, neighbours):
    rows_dev = descriptors.shape[0]
    blocks_dev = rows_dev // BLK
    columns = query_descriptors.shape[0]
    place = lax.axis_index("gal")
    first = place * blocks_dev
    base = first - blocks_dev
    window = padded(descriptors, (("gal", 0),), rows_dev)
    window_blocks = window.reshape(3 * blocks_dev, BLK, D)
    own_row = tile_blocks[:, 0] - first
    win_col = tile_blocks[:, 1] - base
    tiles = build_tiles(window_blocks, own_row + blocks_dev, win_col, neighbours)
    row_hot = (own_row[:, None] == jnp.arange(blocks_dev, dtype=jnp.int32)[None, :]).astype(
        jnp.float32
    )
    row_degree = jnp.einsum(
        "tr,ti->ri", row_hot, jnp.sum(tiles, axis=2), precision=lax.Precision.HIGHEST
    ).reshape(rows_dev)
    col_hot = (win_col[:, None] == jnp.arange(3 * blocks_dev, dtype=jnp.int32)[None, :]).astype(
        jnp.float32
    )
    col_spread = jnp.einsum(
        "tw,ti->wi", col_hot, jnp.sum(tiles, axis=1), precision=lax.Precision.HIGHEST
    )
    degree = 1.0 + (row_degree + send_back(col_spread.reshape(3 * rows_dev), rows_dev))
    scale = 1.0 / jnp.sqrt(degree)
    seed_dots = lax.dot_general(
        descriptors, query_descriptors, (((1,), (1,)), ((), ())), preferred_element_type=jnp.float32
    )
    seeds = jax.nn.softplus(seed_dots / math.sqrt(D))
    ranking = jnp.zeros_like(seeds)
    residual = seeds
    direction = seeds
    norm_now = column_squares(residual)
    for step in range(ITERS):
        scaled = direction * scale[:, None]
        window_field = padded(scaled, (("gal", 0),), rows_dev)
        field_blocks = window_field.reshape(3 * blocks_dev, BLK, columns)
        forward = jnp.einsum(
            "tij,tjq->tiq", tiles, field_blocks[win_col], precision=lax.Precision.HIGHEST
        )
        total = jnp.einsum(
            "tr,tiq->riq", row_hot, forward, precision=lax.Precision.HIGHEST
        ).reshape(rows_dev, columns)
        own_blocks = scaled.reshape(blocks_dev, BLK, columns)
        backward = jnp.einsum(
            "tij,tiq->tjq", tiles, own_blocks[own_row], precision=lax.Precision.HIGHEST
        )
        spread = jnp.einsum("tw,tjq->wjq", col_hot, backward, precision=lax.Precision.HIGHEST)
        total = total + send_back(spread.reshape(3 * rows_dev, columns), rows_dev)
        image = direction - damping * scale[:, None] * total
        alpha = norm_now / lax.psum(jnp.sum(direction * image, axis=0), "gal")
        ranking = ranking + alpha * direction
        residual = residual - alpha * image
        norm_next = column_squares(residual)
        direction = residual + norm_next / norm_now * direction
        norm_now = norm_next
    return (ranking, residual)


def solution(mesh):
    placed = (P("gal", None), P("qry", None), P("gal", None), P("gal", None, None))
    return jax.shard_map(
        per_device,
        mesh=mesh,
        in_specs=placed,
        out_specs=(P("gal", "qry"), P("gal", "qry")),
        check_vma=False,
    )
```

profile of v0, /device:TPU:0, one launch (start us, length us, event | category | flops | bytes accessed | tf_op | source)
XLA Modules:
  0.0 527.7 jit_solution(12158052241159046318)
XLA Ops:
  2.1 6.8 %collective-permute-start = (bf16[2048,512]{1,0:T(8,128)(2,1)}, bf16[2048,512]{1,0:T(8,128)(2,1)}, u32[]{:S(2)}, u32[]{:S(2)}) collective-permute-start(bf16[2048,512]{1,0:T(8,128)(2,1)} %param.4), channel_id=1, source_target_pairs={{0,4},{4,8},{8,12},{12,16},{16,20},{20,24},{24,28},{1,5},{5,9},{9,... | collective-permute-start | bytes 6291464 | tf_op jit(solution)/shard_map/ppermute | solution.py:30
  10.7 40.8 %collective-permute-done.1 = bf16[2048,512]{1,0:T(8,128)(2,1)S(1)} collective-permute-done((bf16[2048,512]{1,0:T(8,128)(2,1)}, bf16[2048,512]{1,0:T(8,128)(2,1)S(1)}, u32[]{:S(2)}, u32[]{:S(2)}) %collective-permute-start.1) | collective-permute-done | bytes 2097184 | tf_op jit(solution)/shard_map/ppermute | solution.py:31
  51.5 45.2 %collective-permute-done = bf16[2048,512]{1,0:T(8,128)(2,1)} collective-permute-done((bf16[2048,512]{1,0:T(8,128)(2,1)}, bf16[2048,512]{1,0:T(8,128)(2,1)}, u32[]{:S(2)}, u32[]{:S(2)}) %collective-permute-start) | collective-permute-done | bytes 2097184 | tf_op jit(solution)/shard_map/ppermute | solution.py:30
  96.7 5.5 %pad_maximum_fusion = bf16[6144,512]{1,0:T(8,128)(2,1)} fusion(bf16[2048,512]{1,0:T(8,128)(2,1)S(1)} %collective-permute-done.1, bf16[2048,512]{1,0:T(8,128)(2,1)} %param.4, bf16[2048,512]{1,0:T(8,128)(2,1)} %collective-permute-done), kind=kLoop, calls=%fused_computation.9 | loop fusion | flops 18874368 | bytes 12582912 | tf_op jit(solution)/shard_map/concatenate | solution.py:32
  102.1 8.3 %gather_fusion = bf16[64,128,512]{2,1,0:T(8,128)(2,1)} fusion(bf16[48,128,512]{2,1,0:T(8,128)(2,1)} %bitcast.137, s32[1024]{0:T(1024)S(1)} %get-tuple-element.55), kind=kCustom, calls=%fused_computation | custom fusion | bytes 16777472 | tf_op jit(solution)/shard_map/gather | solution.py:37
  110.4 8.3 %gather_fusion.1 = bf16[64,128,512]{2,1,0:T(8,128)(2,1)} fusion(bf16[48,128,512]{2,1,0:T(8,128)(2,1)} %bitcast.138, s32[1024]{0:T(1024)S(1)} %get-tuple-element.54), kind=kCustom, calls=%fused_computation.1 | custom fusion | bytes 16777472 | tf_op jit(solution)/shard_map/gather | solution.py:38
  118.7 18.5 %fusion.52 = (f32[64,128]{1,0:T(8,128)S(1)}, f32[64,128]{1,0:T(8,128)S(1)}, f32[64,128,128]{2,1,0:T(8,128)}) fusion(bf16[64,128,512]{2,1,0:T(8,128)(2,1)} %gather_fusion, bf16[64,128,512]{2,1,0:T(8,128)(2,1)} %gather_fusion.1, s32[64,128]{1,0:T(8,128)S(1)} %get-tuple-element.38, s32[64,128]{1,0:T(8,128)S(1)} %get-tuple-element.39, ...), kind=kOutput, calls=%fused_computation.118 | convolution fusion | flops 1120911360 | bytes 21430272 | tf_op jit(solution)/shard_map/tid,tjd->tij/dot_general | solution.py:39
  137.4 4.4 collective-permute-start.3
  143.2 4.2 collective-permute-done.2
  149.7 5.7 %collective-permute-start.4 = (f32[2048,128]{1,0:T(8,128)S(1)}, f32[2048,128]{1,0:T(8,128)}, u32[]{:S(2)}, u32[]{:S(2)}) collective-permute-start(f32[2048,128]{1,0:T(8,128)S(1)} %get-tuple-element.50), channel_id=1, source_target_pairs={{0,4},{4,8},{8,12},{12,16},{16,20},{20,24},{24,28},{1,5},{5,9},{9,... | collective-permute-start | bytes 3145736 | tf_op jit(solution)/shard_map/ppermute | solution.py:30
  155.4 2.8 gather_fusion.3
  158.2 9.2 %fusion.60 = f32[64,128,128]{2,1,0:T(8,128)S(1)} fusion(f32[64,128,128]{2,1,0:T(8,128)} %get-tuple-element.49, f32[64,128,128]{2,1,0:T(8,128)} %gather_fusion.3), kind=kOutput, calls=%fused_computation.123 | convolution fusion | flops 1610612736 | bytes 12582912 | tf_op jit(solution)/shard_map/tij,tiq->tjq/dot_general | solution.py:107
  167.4 4.6 fusion.9
  173.6 4.3 collective-permute-start.7
  181.0 37.9 %collective-permute-done.4 = f32[2048,128]{1,0:T(8,128)} collective-permute-done((f32[2048,128]{1,0:T(8,128)S(1)}, f32[2048,128]{1,0:T(8,128)}, u32[]{:S(2)}, u32[]{:S(2)}) %collective-permute-start.4) | collective-permute-done | bytes 1048608 | tf_op jit(solution)/shard_map/ppermute | solution.py:30
  218.9 3.4 pad_maximum_fusion.1
  222.3 4.6 gather_fusion.2
  227.0 6.7 %fusion.59 = f32[64,128,128]{2,1,0:T(8,128)S(1)} fusion(f32[64,128,128]{2,1,0:T(8,128)} %get-tuple-element.49, f32[64,128,128]{2,1,0:T(8,128)} %gather_fusion.2), kind=kOutput, calls=%fused_computation.122 | convolution fusion | flops 1610612736 | bytes 12582912 | tf_op jit(solution)/shard_map/tij,tjq->tiq/dot_general | solution.py:100
  233.7 3.8 fusion.11
  237.9 3.5 collective-permute-done.7
  243.3 19.6 %all-reduce = (f32[128]{0:T(128)S(1)}, f32[128]{0:T(128)S(1)}) all-reduce(f32[128]{0:T(128)S(1)} %get-tuple-element.5, f32[128]{0:T(128)S(1)} %get-tuple-element.4), channel_id=1, replica_groups=mesh['gal'=8,'qry'=4] {'gal'}, use_global_device_ids=true, to_apply=%region_1.2 | all-reduce | flops 256 | bytes 2048 | tf_op jit(solution)/shard_map/psum | solution.py:59
  263.3 17.2 %psum.44 = f32[128]{0:T(128)S(1)} all-reduce(f32[128]{0:T(128)S(1)} %multiply_reduce_fusion.3), channel_id=1, replica_groups=mesh['gal'=8,'qry'=4] {'gal'}, use_global_device_ids=true, to_apply=%region_7.8 | all-reduce | flops 128 | bytes 1024 | tf_op jit(solution)/shard_map/psum | solution.py:59
  283.4 5.9 %collective-permute-start.8 = (f32[2048,128]{1,0:T(8,128)S(1)}, f32[2048,128]{1,0:T(8,128)}, u32[]{:S(2)}, u32[]{:S(2)}) collective-permute-start(f32[2048,128]{1,0:T(8,128)S(1)} %get-tuple-element.16), channel_id=1, source_target_pairs={{0,4},{4,8},{8,12},{12,16},{16,20},{20,24},{24,28},{1,5},{5,9},{9,... | collective-permute-start | bytes 3145736 | tf_op jit(solution)/shard_map/ppermute | solution.py:30
  292.0 9.2 %fusion.62 = f32[64,128,128]{2,1,0:T(8,128)S(1)} fusion(f32[64,128,128]{2,1,0:T(8,128)} %get-tuple-element.49, f32[64,128,128]{2,1,0:T(8,128)} %gather_fusion.5), kind=kOutput, calls=%fused_computation.125 | convolution fusion | flops 1610612736 | bytes 12582912 | tf_op jit(solution)/shard_map/tij,tiq->tjq/dot_general | solution.py:107
  301.3 4.5 fusion.5
  307.4 4.8 collective-permute-start.11
  316.3 31.1 %collective-permute-done.8 = f32[2048,128]{1,0:T(8,128)} collective-permute-done((f32[2048,128]{1,0:T(8,128)S(1)}, f32[2048,128]{1,0:T(8,128)}, u32[]{:S(2)}, u32[]{:S(2)}) %collective-permute-start.8) | collective-permute-done | bytes 1048608 | tf_op jit(solution)/shard_map/ppermute | solution.py:30
  347.3 3.4 pad_maximum_fusion.2
  350.8 4.6 gather_fusion.4
  355.4 6.7 %fusion.61 = f32[64,128,128]{2,1,0:T(8,128)S(1)} fusion(f32[64,128,128]{2,1,0:T(8,128)} %get-tuple-element.49, f32[64,128,128]{2,1,0:T(8,128)} %gather_fusion.4), kind=kOutput, calls=%fused_computation.124 | convolution fusion | flops 1610612736 | bytes 12582912 | tf_op jit(solution)/shard_map/tij,tjq->tiq/dot_general | solution.py:100
  362.1 3.8 fusion.7
  366.3 3.5 collective-permute-done.11
  369.9 2.9 multiply_reduce_fusion.2
  372.7 19.6 %psum.45 = f32[128]{0:T(128)S(1)} all-reduce(f32[128]{0:T(128)S(1)} %get-tuple-element.14), channel_id=1, replica_groups=mesh['gal'=8,'qry'=4] {'gal'}, use_global_device_ids=true, to_apply=%region_9.10 | all-reduce | flops 128 | bytes 1024 | tf_op jit(solution)/shard_map/psum | solution.py:113
  394.7 17.2 %psum.46 = f32[128]{0:T(128)S(1)} all-reduce(f32[128]{0:T(128)S(1)} %get-tuple-element.12), channel_id=1, replica_groups=mesh['gal'=8,'qry'=4] {'gal'}, use_global_device_ids=true, to_apply=%region_11.12 | all-reduce | flops 128 | bytes 1024 | tf_op jit(solution)/shard_map/psum | solution.py:59
  415.7 5.7 %collective-permute-start.12 = (f32[2048,128]{1,0:T(8,128)S(1)}, f32[2048,128]{1,0:T(8,128)}, u32[]{:S(2)}, u32[]{:S(2)}) collective-permute-start(f32[2048,128]{1,0:T(8,128)S(1)} %get-tuple-element.10), channel_id=1, source_target_pairs={{0,4},{4,8},{8,12},{12,16},{16,20},{20,24},{24,28},{1,5},{5,9},{9,... | collective-permute-start | bytes 3145736 | tf_op jit(solution)/shard_map/ppermute | solution.py:30
  424.2 9.2 %fusion.64 = f32[64,128,128]{2,1,0:T(8,128)S(1)} fusion(f32[64,128,128]{2,1,0:T(8,128)} %get-tuple-element.49, f32[64,128,128]{2,1,0:T(8,128)} %gather_fusion.7), kind=kOutput, calls=%fused_computation.127 | convolution fusion | flops 1610612736 | bytes 12582912 | tf_op jit(solution)/shard_map/tij,tiq->tjq/dot_general | solution.py:107
  433.4 4.6 fusion.1
  439.5 4.8 collective-permute-start.15
  448.4 30.8 %collective-permute-done.12 = f32[2048,128]{1,0:T(8,128)} collective-permute-done((f32[2048,128]{1,0:T(8,128)S(1)}, f32[2048,128]{1,0:T(8,128)}, u32[]{:S(2)}, u32[]{:S(2)}) %collective-permute-start.12) | collective-permute-done | bytes 1048608 | tf_op jit(solution)/shard_map/ppermute | solution.py:30
  479.3 3.4 pad_maximum_fusion.3
  482.7 4.6 gather_fusion.6
  487.3 6.7 %fusion.63 = f32[64,128,128]{2,1,0:T(8,128)S(1)} fusion(f32[64,128,128]{2,1,0:T(8,128)} %get-tuple-element.49, f32[64,128,128]{2,1,0:T(8,128)} %gather_fusion.6), kind=kOutput, calls=%fused_computation.126 | convolution fusion | flops 1610612736 | bytes 12582912 | tf_op jit(solution)/shard_map/tij,tjq->tiq/dot_general | solution.py:100
  494.0 3.8 fusion.3
  498.3 3.5 collective-permute-done.15
  501.7 3.0 multiply_reduce_fusion
  504.7 19.6 %psum.47 = f32[128]{0:T(128)S(1)} all-reduce(f32[128]{0:T(128)S(1)} %get-tuple-element.8), channel_id=1, replica_groups=mesh['gal'=8,'qry'=4] {'gal'}, use_global_device_ids=true, to_apply=%region_13.14 | all-reduce | flops 128 | bytes 1024 | tf_op jit(solution)/shard_map/psum | solution.py:113
  524.3 3.1 multiply_subtract_fusion
  (68 shorter events, 40.8 us)
Async XLA Ops:
  0.6 146.9 %copy-start = (bf16[128,512]{1,0:T(8,128)(2,1)S(1)}, bf16[128,512]{1,0:T(8,128)(2,1)}, u32[]{:S(2)}) copy-start(bf16[128,512]{1,0:T(8,128)(2,1)} %param.5) | copy-start | bytes 393220
  0.6 50.8 %collective-permute-start.1 = (bf16[2048,512]{1,0:T(8,128)(2,1)}, bf16[2048,512]{1,0:T(8,128)(2,1)S(1)}, u32[]{:S(2)}, u32[]{:S(2)}) collective-permute-start(bf16[2048,512]{1,0:T(8,128)(2,1)} %param.4), channel_id=1, source_target_pairs={{4,0},{8,4},{12,8},{16,12},{20,16},{24,20},{28,24},{5,1},{9,5},{13... | collective-permute-start | bytes 6291464 | tf_op jit(solution)/shard_map/ppermute | solution.py:31
  2.1 94.6 %collective-permute-start = (bf16[2048,512]{1,0:T(8,128)(2,1)}, bf16[2048,512]{1,0:T(8,128)(2,1)}, u32[]{:S(2)}, u32[]{:S(2)}) collective-permute-start(bf16[2048,512]{1,0:T(8,128)(2,1)} %param.4), channel_id=1, source_target_pairs={{0,4},{4,8},{8,12},{12,16},{16,20},{20,24},{24,28},{1,5},{5,9},{9,... | collective-permute-start | bytes 6291464 | tf_op jit(solution)/shard_map/ppermute | solution.py:30
  118.7 28.8 %copy-start.8 = (bf16[2048,512]{1,0:T(8,128)(2,1)S(1)}, bf16[2048,512]{1,0:T(8,128)(2,1)}, u32[]{:S(2)}) copy-start(bf16[2048,512]{1,0:T(8,128)(2,1)} %param.4) | copy-start | bytes 6291460
  137.4 5.7 %collective-permute-start.3 = (f32[2048]{0:T(1024)S(1)}, f32[2048]{0:T(1024)S(1)}, u32[]{:S(2)}, u32[]{:S(2)}) collective-permute-start(f32[2048]{0:T(1024)S(1)} %get-tuple-element.41), channel_id=1, source_target_pairs={{0,4},{4,8},{8,12},{12,16},{16,20},{20,24},{24,28},{1,5},{5,9},{9,... | collective-permute-start | bytes 24584 | tf_op jit(solution)/shard_map/ppermute | solution.py:20
  141.8 5.5 %collective-permute-start.2 = (f32[2048]{0:T(1024)S(1)}, f32[2048]{0:T(1024)S(1)}, u32[]{:S(2)}, u32[]{:S(2)}) collective-permute-start(f32[2048]{0:T(1024)S(1)} %get-tuple-element.40), channel_id=1, source_target_pairs={{4,0},{8,4},{12,8},{16,12},{20,16},{24,20},{28,24},{5,1},{9,5},{13... | collective-permute-start | bytes 24584 | tf_op jit(solution)/shard_map/ppermute | solution.py:20
  148.4 32.6 %collective-permute-start.5 = (f32[2048,128]{1,0:T(8,128)S(1)}, f32[2048,128]{1,0:T(8,128)}, u32[]{:S(2)}, u32[]{:S(2)}) collective-permute-start(f32[2048,128]{1,0:T(8,128)S(1)} %get-tuple-element.50), channel_id=1, source_target_pairs={{4,0},{8,4},{12,8},{16,12},{20,16},{24,20},{28,24},{5,1},{9,5},{13... | collective-permute-start | bytes 3145736 | tf_op jit(solution)/shard_map/ppermute | solution.py:31
  149.7 69.2 %collective-permute-start.4 = (f32[2048,128]{1,0:T(8,128)S(1)}, f32[2048,128]{1,0:T(8,128)}, u32[]{:S(2)}, u32[]{:S(2)}) collective-permute-start(f32[2048,128]{1,0:T(8,128)S(1)} %get-tuple-element.50), channel_id=1, source_target_pairs={{0,4},{4,8},{8,12},{12,16},{16,20},{20,24},{24,28},{1,5},{5,9},{9,... | collective-permute-start | bytes 3145736 | tf_op jit(solution)/shard_map/ppermute | solution.py:30
  173.6 67.8 %collective-permute-start.7 = (f32[2048,128]{1,0:T(8,128)}, f32[2048,128]{1,0:T(8,128)}, u32[]{:S(2)}, u32[]{:S(2)}) collective-permute-start(f32[2048,128]{1,0:T(8,128)} %bitcast.29), channel_id=1, source_target_pairs={{0,4},{4,8},{8,12},{12,16},{16,20},{20,24},{24,28},{1,5},{5,9},{9,... | collective-permute-start | bytes 3145736 | tf_op jit(solution)/shard_map/ppermute | solution.py:20
  179.2 62.2 %collective-permute-start.6 = (f32[2048,128]{1,0:T(8,128)}, f32[2048,128]{1,0:T(8,128)}, u32[]{:S(2)}, u32[]{:S(2)}) collective-permute-start(f32[2048,128]{1,0:T(8,128)} %bitcast.28), channel_id=1, source_target_pairs={{4,0},{8,4},{12,8},{16,12},{20,16},{24,20},{28,24},{5,1},{9,5},{13... | collective-permute-start | bytes 3145736 | tf_op jit(solution)/shard_map/ppermute | solution.py:20
  243.3 37.2 %copy-start.2 = (f32[2048,128]{1,0:T(8,128)}, f32[2048,128]{1,0:T(8,128)S(1)}, u32[]{:S(2)}) copy-start(f32[2048,128]{1,0:T(8,128)S(1)} %get-tuple-element.18) | copy-start | bytes 3145732
  282.1 34.2 %collective-permute-start.9 = (f32[2048,128]{1,0:T(8,128)S(1)}, f32[2048,128]{1,0:T(8,128)}, u32[]{:S(2)}, u32[]{:S(2)}) collective-permute-start(f32[2048,128]{1,0:T(8,128)S(1)} %get-tuple-element.16), channel_id=1, source_target_pairs={{4,0},{8,4},{12,8},{16,12},{20,16},{24,20},{28,24},{5,1},{9,5},{13... | collective-permute-start | bytes 3145736 | tf_op jit(solution)/shard_map/ppermute | solution.py:31
  283.4 64.0 %collective-permute-start.8 = (f32[2048,128]{1,0:T(8,128)S(1)}, f32[2048,128]{1,0:T(8,128)}, u32[]{:S(2)}, u32[]{:S(2)}) collective-permute-start(f32[2048,128]{1,0:T(8,128)S(1)} %get-tuple-element.16), channel_id=1, source_target_pairs={{0,4},{4,8},{8,12},{12,16},{16,20},{20,24},{24,28},{1,5},{5,9},{9,... | collective-permute-start | bytes 3145736 | tf_op jit(solution)/shard_map/ppermute | solution.py:30
  307.4 62.4 %collective-permute-start.11 = (f32[2048,128]{1,0:T(8,128)}, f32[2048,128]{1,0:T(8,128)}, u32[]{:S(2)}, u32[]{:S(2)}) collective-permute-start(f32[2048,128]{1,0:T(8,128)} %bitcast.35), channel_id=1, source_target_pairs={{0,4},{4,8},{8,12},{12,16},{16,20},{20,24},{24,28},{1,5},{5,9},{9,... | collective-permute-start | bytes 3145736 | tf_op jit(solution)/shard_map/ppermute | solution.py:20
  313.5 56.4 %collective-permute-start.10 = (f32[2048,128]{1,0:T(8,128)}, f32[2048,128]{1,0:T(8,128)}, u32[]{:S(2)}, u32[]{:S(2)}) collective-permute-start(f32[2048,128]{1,0:T(8,128)} %bitcast.34), channel_id=1, source_target_pairs={{4,0},{8,4},{12,8},{16,12},{20,16},{24,20},{28,24},{5,1},{9,5},{13... | collective-permute-start | bytes 3145736 | tf_op jit(solution)/shard_map/ppermute | solution.py:20
  362.1 7.7 %copy-start.7 = (f32[16,128,128]{2,1,0:T(8,128)S(1)}, f32[16,128,128]{2,1,0:T(8,128)}, u32[]{:S(2)}) copy-start(f32[16,128,128]{2,1,0:T(8,128)} %copy.11) | copy-start | bytes 3145732
  366.0 26.3 %copy-start.3 = (f32[2048,128]{1,0:T(8,128)S(1)}, f32[2048,128]{1,0:T(8,128)}, u32[]{:S(2)}) copy-start(f32[2048,128]{1,0:T(8,128)} %copy-done.2) | copy-start | bytes 3145732
  414.4 34.0 %collective-permute-start.13 = (f32[2048,128]{1,0:T(8,128)S(1)}, f32[2048,128]{1,0:T(8,128)}, u32[]{:S(2)}, u32[]{:S(2)}) collective-permute-start(f32[2048,128]{1,0:T(8,128)S(1)} %get-tuple-element.10), channel_id=1, source_target_pairs={{4,0},{8,4},{12,8},{16,12},{20,16},{24,20},{28,24},{5,1},{9,5},{13... | collective-permute-start | bytes 3145736 | tf_op jit(solution)/shard_map/ppermute | solution.py:31
  415.7 63.6 %collective-permute-start.12 = (f32[2048,128]{1,0:T(8,128)S(1)}, f32[2048,128]{1,0:T(8,128)}, u32[]{:S(2)}, u32[]{:S(2)}) collective-permute-start(f32[2048,128]{1,0:T(8,128)S(1)} %get-tuple-element.10), channel_id=1, source_target_pairs={{0,4},{4,8},{8,12},{12,16},{16,20},{20,24},{24,28},{1,5},{5,9},{9,... | collective-permute-start | bytes 3145736 | tf_op jit(solution)/shard_map/ppermute | solution.py:30
  439.5 62.2 %collective-permute-start.15 = (f32[2048,128]{1,0:T(8,128)}, f32[2048,128]{1,0:T(8,128)}, u32[]{:S(2)}, u32[]{:S(2)}) collective-permute-start(f32[2048,128]{1,0:T(8,128)} %bitcast.41), channel_id=1, source_target_pairs={{0,4},{4,8},{8,12},{12,16},{16,20},{20,24},{24,28},{1,5},{5,9},{9,... | collective-permute-start | bytes 3145736 | tf_op jit(solution)/shard_map/ppermute | solution.py:20
  445.6 56.2 %collective-permute-start.14 = (f32[2048,128]{1,0:T(8,128)}, f32[2048,128]{1,0:T(8,128)}, u32[]{:S(2)}, u32[]{:S(2)}) collective-permute-start(f32[2048,128]{1,0:T(8,128)} %bitcast.40), channel_id=1, source_target_pairs={{4,0},{8,4},{12,8},{16,12},{20,16},{24,20},{28,24},{5,1},{9,5},{13... | collective-permute-start | bytes 3145736 | tf_op jit(solution)/shard_map/ppermute | solution.py:20
  494.0 7.7 %copy-start.5 = (f32[2048,128]{1,0:T(8,128)S(1)}, f32[2048,128]{1,0:T(8,128)}, u32[]{:S(2)}) copy-start(f32[2048,128]{1,0:T(8,128)} %get-tuple-element.11) | copy-start | bytes 3145732
  494.0 7.7 %copy-start.6 = (f32[16,128,128]{2,1,0:T(8,128)S(1)}, f32[16,128,128]{2,1,0:T(8,128)}, u32[]{:S(2)}) copy-start(f32[16,128,128]{2,1,0:T(8,128)} %copy.15) | copy-start | bytes 3145732
  497.9 26.4 %copy-start.4 = (f32[2048,128]{1,0:T(8,128)S(1)}, f32[2048,128]{1,0:T(8,128)}, u32[]{:S(2)}) copy-start(f32[2048,128]{1,0:T(8,128)} %get-tuple-element.13) | copy-start | bytes 3145732
  501.7 25.7 %copy-start.1 = (bf16[128,512]{1,0:T(8,128)(2,1)S(1)}, bf16[128,512]{1,0:T(8,128)(2,1)}, u32[]{:S(2)}) copy-start(bf16[128,512]{1,0:T(8,128)(2,1)} %param.5) | copy-start | bytes 393220
where the time goes:
time: 533 us; the launch traced here: 528 us
  waiting for transfers between devices  201 us (38%)
  blocking collectives  93.3 us (18%)
  matrix products  92.7 us (17%)
  starting transfers between devices  53.4 us (10%)
  local copies, waits for them, and re-layouts  52.3 us (10%)
  other arithmetic  34.1 us (6%)
    ppermute x4, waiting for transfers between devices, padded(): before = lax.ppermute(last, axis, up)  145 us
    psum x3, blocking collectives, column_squares(): return lax.psum(jnp.sum(current * current, axis=0), 'gal')  54.1 us
    ppermute x4, waiting for transfers between devices, padded(): after = lax.ppermute(leading, axis, down)  40.8 us
    psum x2, blocking collectives, per_device(): alpha = norm_now / lax.psum(jnp.sum(direction * image, axis=0), 'gal')  39.2 us
    dot_general x3, matrix products, per_device(): jnp.einsum('tij,tiq->tjq', tiles, own_blocks[own_row], precision=lax.Prec...  27.7 us
    ppermute x4, starting transfers between devices, padded(): before = lax.ppermute(last, axis, up)  24.1 us
    ppermute x8, starting transfers between devices, from_behind(): lax.ppermute(value, axis, [(source, source + steps) for source in range(l...  24 us
    dot_general x3, matrix products, per_device(): jnp.einsum('tij,tjq->tiq', tiles, field_blocks[win_col], precision=lax.Pr...  20.1 us
  transfers between devices with their start and end apart: 16, of which 9 were waited for; matrix products, arithmetic and copies ran while one was open for 23% of the time, Pallas kernels for 0%

commit v1 on v0

v1 whole, which is shorter than its diff:
```python
import functools
import math

import jax
import jax.numpy as jnp
from jax import lax
from jax.experimental import pallas as pl
from jax.experimental.pallas import tpu as pltpu
from jax.sharding import PartitionSpec as P

BLK = 128
DAMPING = 0.99
STAGE = 4
CHUNK = 16
VMEM_LIMIT = 60 * 1024 * 1024


def softplus(value):
    return jnp.maximum(value, 0.0) + jnp.log1p(jnp.exp(-jnp.abs(value)))


def build_kernel(tiles, entries, blocks, row_ref, col_ref, window_ref, near_ref,
                 mats_ref, degree_ref, dst_ref, src_ref, count_ref, stage, sems):
    root = 1.0 / math.sqrt(window_ref.shape[1])
    degree_ref[...] = jnp.zeros_like(degree_ref)
    count_ref[0] = 0
    count_ref[1] = 0
    places = lax.broadcasted_iota(jnp.int32, (BLK, BLK), 0).astype(jnp.float32)

    def emit(mat, slot, dst, src):
        sent = count_ref[0]
        place = lax.rem(sent, STAGE)

        @pl.when(sent >= STAGE)
        def _():
            pltpu.make_async_copy(stage.at[place], mats_ref.at[0], sems.at[place]).wait()

        high = mat.astype(jnp.bfloat16)
        stage[place, :, 0:BLK] = high
        stage[place, :, BLK:] = (mat - high.astype(jnp.float32)).astype(jnp.bfloat16)
        pltpu.make_async_copy(stage.at[place], mats_ref.at[slot], sems.at[place]).start()
        count_ref[0] = sent + 1
        dst_ref[slot] = dst
        src_ref[slot] = src
        rows = pl.ds(pl.multiple_of(dst * BLK, BLK), BLK)
        degree_ref[rows, :] += jnp.broadcast_to(jnp.sum(mat, axis=1, keepdims=True), (BLK, BLK))

    def turned(t):
        left = window_ref[pl.ds(pl.multiple_of(row_ref[t] * BLK, BLK), BLK), :]
        right = window_ref[pl.ds(pl.multiple_of(col_ref[t] * BLK, BLK), BLK), :]
        dots = lax.dot_general(right, left, (((1,), (1,)), ((), ())),
                               preferred_element_type=jnp.float32)
        near = near_ref[t].astype(jnp.float32)
        counted = jnp.zeros((BLK, BLK), jnp.float32)
        for k in range(entries):
            counted += jnp.where(places == near[k:k + 1, :], 1.0, 0.0)
        return counted * softplus(dots * root)

    def mine(t):
        col = col_ref[t]
        return jnp.logical_and(col >= blocks, col < 2 * blocks)

    def emit_back(t, mat):
        slot = tiles + count_ref[1]
        emit(mat, slot, col_ref[t] - blocks, row_ref[t])
        count_ref[1] = slot - tiles + 1

    @pl.loop(0, tiles)
    def _(t):
        mat = turned(t)
        emit(mat.T, t, row_ref[t] - blocks, col_ref[t])

        @pl.when(mine(t))
        def _():
            emit_back(t, mat)

    @pl.loop(tiles, 3 * tiles)
    def _(t):
        @pl.when(mine(t))
        def _():
            emit_back(t, turned(t))

    for place in range(STAGE):
        pltpu.make_async_copy(stage.at[place], mats_ref.at[0], sems.at[place]).wait()


def build(row, col, window, near):
    total, entries, _ = near.shape
    tiles = total // 3
    blocks = window.shape[0] // (3 * BLK)
    smem = pl.BlockSpec(memory_space=pltpu.SMEM)
    vmem = pl.BlockSpec(memory_space=pltpu.VMEM)
    return pl.pallas_call(
        functools.partial(build_kernel, tiles, entries, blocks),
        out_shape=(
            jax.ShapeDtypeStruct((4 * tiles, BLK, 2 * BLK), jnp.bfloat16),
            jax.ShapeDtypeStruct((blocks * BLK, BLK), jnp.float32),
            jax.ShapeDtypeStruct((4 * tiles,), jnp.int32),
            jax.ShapeDtypeStruct((4 * tiles,), jnp.int32),
            jax.ShapeDtypeStruct((2,), jnp.int32),
        ),
        in_specs=[smem, smem, vmem, vmem],
        out_specs=(pl.BlockSpec(memory_space=pl.ANY), vmem, smem, smem, smem),
        scratch_shapes=[
            pltpu.VMEM((STAGE, BLK, 2 * BLK), jnp.bfloat16),
            pltpu.SemaphoreType.DMA((STAGE,)),
        ],
        compiler_params=pltpu.CompilerParams(vmem_limit_bytes=VMEM_LIMIT),
        name="build_tiles",
    )(row, col, window, near)


def step_kernel(step, blocks, tiles, *refs):
    refs = list(refs)

    def take(count):
        taken = refs[:count]
        del refs[:count]
        return taken

    dst_ref, src_ref, count_ref, mats_ref, scale_ref = take(5)
    if step == 0:
        dir_in, halo_in = take(2)
        res_in = dir_in
    else:
        sums_in, res_in, dir_in, image_in = take(4)
        if step == 1:
            (halo_in,) = take(1)
            tail_in = halo_in
        else:
            halo_in, tail_in = take(2)
        fresh_low, fresh_high = take(2)
    if step > 0:
        res_out, dir_out = take(2)
    image_out, sums_out = take(2)
    if step < 2:
        (send_out,) = take(1)
    if step == 1:
        halo_out, tail_out = take(2)
    mats, field, total, sems = refs

    chunks = mats.shape[0] // CHUNK
    used = tiles + count_ref[1]

    def fetch(c):
        span = pl.ds(c * CHUNK, CHUNK)
        return pltpu.make_async_copy(mats_ref.at[span], mats.at[span], sems.at[c])

    for c in range(chunks):
        @pl.when(c * CHUNK < used)
        def _():
            fetch(c).start()

    total[...] = jnp.zeros_like(total)
    sums_out[...] = jnp.zeros_like(sums_out)
    if step > 0:
        norm = sums_in[0:1, :]
        alpha = norm / sums_in[1:2, :]
        after = norm - 2.0 * alpha * sums_in[2:3, :] + alpha * alpha * sums_in[3:4, :]
        beta = after / norm

    def put(block, value):
        high = value.astype(jnp.bfloat16)
        low = (value - high.astype(jnp.float32)).astype(jnp.bfloat16)
        field[block, 0:BLK, 0:BLK] = high
        field[block, 0:BLK, BLK:] = low
        field[block, BLK:, 0:BLK] = high
        field[block, BLK:, BLK:] = low

    def rows_of(b):
        return pl.ds(pl.multiple_of(b * BLK, BLK), BLK)

    @pl.loop(0, blocks)
    def _(b):
        rows = rows_of(b)
        direction = dir_in[rows, :]
        if step > 0:
            residual = res_in[rows, :] - alpha * image_in[rows, :]
            direction = residual + beta * direction
            res_out[rows, :] = residual
            dir_out[rows, :] = direction
        put(blocks + b, direction * scale_ref[rows, :])
        for half in range(2):
            here = rows_of(half * blocks + b)
            value = halo_in[here, :]
            if step > 0:
                fresh = (fresh_low, fresh_high)[half][rows, :]
                tail = tail_in[here, :] - alpha * fresh
                value = tail + beta * value
                if step == 1:
                    halo_out[here, :] = value
                    tail_out[here, :] = tail
            put(2 * half * blocks + b, value)

    def partial(n):
        both = jnp.dot(mats[n], field[src_ref[n]], preferred_element_type=jnp.float32)
        return both[:, 0:BLK] + both[:, BLK:]

    def run(first, count):
        terms = [partial(first + i) for i in range(count)]
        for i in range(count):
            total[rows_of(dst_ref[first + i]), :] += terms[i]

    @pl.loop(0, pl.cdiv(used, CHUNK))
    def _(c):
        fetch(c).wait()
        first = c * CHUNK
        have = jnp.minimum(CHUNK, used - first)

        @pl.loop(0, have // 4)
        def _(g):
            run(first + 4 * g, 4)

        @pl.loop(have // 4 * 4, have)
        def _(i):
            run(first + i, 1)

    @pl.loop(0, blocks)
    def _(b):
        rows = rows_of(b)
        scale = scale_ref[rows, :]
        direction = (dir_out if step > 0 else dir_in)[rows, :]
        residual = (res_out if step > 0 else res_in)[rows, :]
        image = direction - DAMPING * scale * total[rows, :]
        image_out[rows, :] = image
        if step < 2:
            send_out[rows, :] = scale * image
        for place, value in enumerate(
            (residual * residual, direction * image, residual * image, image * image)
        ):
            sums_out[place:place + 1, :] += jnp.sum(value, axis=0, keepdims=True)


def run_step(step, dst, src, count, mats, scale, *rest):
    rows, columns = scale.shape[0], rest[-1].shape[1]
    tiles = dst.shape[0] // 4
    blocks = rows // BLK
    smem = pl.BlockSpec(memory_space=pltpu.SMEM)
    vmem = pl.BlockSpec(memory_space=pltpu.VMEM)
    own = jax.ShapeDtypeStruct((rows, columns), jnp.float32)
    twice = jax.ShapeDtypeStruct((2 * rows, columns), jnp.float32)
    sums = jax.ShapeDtypeStruct((8, columns), jnp.float32)
    outs = ([own, own] if step > 0 else []) + [own, sums]
    if step < 2:
        outs += [own]
    if step == 1:
        outs += [twice, twice]
    return pl.pallas_call(
        functools.partial(step_kernel, step, blocks, tiles),
        out_shape=tuple(outs),
        in_specs=[smem, smem, smem, pl.BlockSpec(memory_space=pl.ANY), vmem]
        + [vmem] * len(rest),
        out_specs=tuple(vmem for _ in outs),
        scratch_shapes=[
            pltpu.VMEM(mats.shape, jnp.bfloat16),
            pltpu.VMEM((3 * blocks, 2 * BLK, 2 * BLK), jnp.bfloat16),
            pltpu.VMEM((rows, columns), jnp.float32),
            pltpu.SemaphoreType.DMA((mats.shape[0] // CHUNK,)),
        ],
        compiler_params=pltpu.CompilerParams(vmem_limit_bytes=VMEM_LIMIT),
        name="operator_step",
    )(dst, src, count, mats, scale, *rest)


def from_sides(value):
    count = lax.axis_size("gal")
    up = [(i, i + 1) for i in range(count - 1)]
    down = [(i + 1, i) for i in range(count - 1)]
    return lax.ppermute(value, "gal", up), lax.ppermute(value, "gal", down)


def per_device(descriptors, query_descriptors, tile_blocks, neighbours):
    rows, width = descriptors.shape
    tiles = tile_blocks.shape[0]
    blocks = rows // BLK
    place = lax.axis_index("gal")
    count = lax.axis_size("gal")
    parts = lax.axis_size("qry")
    part = lax.axis_index("qry")

    def spread(value):
        size = value.shape[0] // parts
        piece = lax.dynamic_slice_in_dim(value, part * size, size, axis=0)
        pieces = jnp.stack(from_sides(piece))
        whole = lax.all_gather(pieces, "qry", axis=1)
        return whole.reshape((2,) + value.shape)

    near = neighbours.astype(jnp.bfloat16)
    beside = spread(descriptors)
    near_beside = spread(near)
    window = jnp.concatenate([beside[0], descriptors, beside[1]], axis=0)
    near_all = jnp.concatenate([near, near_beside[0], near_beside[1]], axis=0)
    below, above = from_sides(tile_blocks)
    base = (place - 1) * blocks
    far = jnp.int32(3 * blocks)
    local = jnp.concatenate([tile_blocks, below, above], axis=0) - base
    origin = jnp.repeat(jnp.array([0, -1, 1], jnp.int32), tiles) + place
    exists = jnp.logical_and(origin >= 0, origin < count)
    row = local[:, 0]
    col = jnp.where(exists, local[:, 1], far)

    mats, degree, dst, src, used = build(row, col, window, near_all)
    scale = 1.0 / jnp.sqrt(1.0 + degree)
    scale_low, scale_high = from_sides(scale[:, 0])
    seeds = jax.nn.softplus(
        lax.dot_general(window, query_descriptors, (((1,), (1,)), ((), ())),
                        preferred_element_type=jnp.float32) / math.sqrt(width)
    )
    own = seeds[rows:2 * rows]
    halo = jnp.concatenate(
        [seeds[:rows] * scale_low[:, None], seeds[2 * rows:] * scale_high[:, None]], axis=0
    )
    image0, sums0, send0 = run_step(0, dst, src, used, mats, scale, own, halo)
    fresh = from_sides(send0)
    sums0 = lax.psum(sums0, "gal")
    res1, dir1, image1, sums1, send1, halo1, tail1 = run_step(
        1, dst, src, used, mats, scale, sums0, own, own, image0, halo, *fresh
    )
    fresh = from_sides(send1)
    sums1 = lax.psum(sums1, "gal")
    res2, dir2, image2, sums2 = run_step(
        2, dst, src, used, mats, scale, sums1, res1, dir1, image1, halo1, tail1, *fresh
    )
    sums2 = lax.psum(sums2, "gal")
    alpha0, alpha1, alpha2 = (s[0:1] / s[1:2] for s in (sums0, sums1, sums2))
    ranking = alpha0 * own + alpha1 * dir1 + alpha2 * dir2
    residual = res2 - alpha2 * image2
    return ranking, residual


def solution(mesh):
    placed = (P("gal", None), P("qry", None), P("gal", None), P("gal", None, None))
    return jax.shard_map(
        per_device,
        mesh=mesh,
        in_specs=placed,
        out_specs=(P("gal", "qry"), P("gal", "qry")),
        check_vma=False,
    )
```

time: 533 us -> 361 us (0.68)
  waiting for transfers between devices: 201 us -> 36.1 us
  matrix products: 92.7 us -> 3.67 us
  Pallas kernels: 0 us -> 84.3 us
  blocking collectives: 93.3 us -> 139 us
  local copies, waits for them, and re-layouts: 52.3 us -> 7.74 us
  between operations: 1.29 us -> 14.4 us
  starting transfers between devices: 53.4 us -> 43.4 us
    ppermute x16 -> x12, waiting for transfers between devices: 201 us -> 26.5 us  [from_sides(): return (lax.ppermute(value, 'gal', up), lax.ppermute(value, 'gal', down))]
    dot_general x16 -> x1, matrix products: 92.7 us -> 3.67 us  [per_device(): lax.dot_general(window, query_descriptors, (((1,), (1,)), ((), ())), pref...]
    pallas_call x0 -> x4, Pallas kernels: none -> 84.3 us  [the longest x3 44.8 us: run_step(): pl.pallas_call(functools.partial(step_kernel, step, blocks, tiles), out_s...]
    gather x8 -> x0, local copies, waits for them, and re-layouts: 38.8 us -> none  [the longest x3 13.9 us: per_device(): field_blocks[win_col]]
    psum x5 -> x3, blocking collectives: 93.3 us -> 128 us  [the longest x1 58 us: per_device(): sums0 = lax.psum(sums0, 'gal')]
    slice x13 -> x2, local copies, waits for them, and re-layouts: 11.5 us -> 0.87 us  [the longest x1 0.53 us: per_device(): col = jnp.where(exists, local[:, 1], far)]
    all_gather x0 -> x1, blocking collectives: none -> 10.4 us  [spread(): whole = lax.all_gather(pieces, 'qry', axis=1)]
    reduce_sum x5 -> x0, other arithmetic: 10.4 us -> none  [the longest x3 7.72 us: per_device(): alpha = norm_now / lax.psum(jnp.sum(direction * image, axis=0), 'gal')]
  transfers between devices with their start and end apart: 16 -> 13, of which waited for: 9 -> 4; matrix products, arithmetic and copies ran while one was open for 23% -> 2% of each run, Pallas kernels for 0% -> 0%
where the time goes in v1:
time: 361 us; the launch traced here: 358 us
  blocking collectives  139 us (39%)
  Pallas kernels  84.3 us (23%)
  starting transfers between devices  43.4 us (12%)
  waiting for transfers between devices  36.1 us (10%)
  other arithmetic  29.7 us (8%)
  between operations  14.4 us (4%)
  local copies, waits for them, and re-layouts  7.74 us (2%)
  matrix products  3.67 us (1%)
    psum x1, blocking collectives, per_device(): sums0 = lax.psum(sums0, 'gal')  58 us
    psum x1, blocking collectives, per_device(): sums1 = lax.psum(sums1, 'gal')  53 us
    pallas_call x3, Pallas kernels, run_step(): pl.pallas_call(functools.partial(step_kernel, step, blocks, tiles), out_s...  44.8 us
    ppermute x12, starting transfers between devices, from_sides(): return (lax.ppermute(value, 'gal', up), lax.ppermute(value, 'gal', down))  43.3 us
    pallas_call x1, Pallas kernels, build(): pl.pallas_call(functools.partial(build_kernel, tiles, entries, blocks), o...  39.5 us
    ppermute x12, waiting for transfers between devices, from_sides(): return (lax.ppermute(value, 'gal', up), lax.ppermute(value, 'gal', down))  26.5 us
    concatenate x1, other arithmetic, per_device(): window = jnp.concatenate([beside[0], descriptors, beside[1]], axis=0)  17.6 us
    psum x1, blocking collectives, per_device(): sums2 = lax.psum(sums2, 'gal')  17.4 us
  transfers between devices with their start and end apart: 13, of which 4 were waited for; matrix products, arithmetic and copies ran while one was open for 2% of the time, Pallas kernels for 0%

profile of v1, /device:TPU:0, one launch (start us, length us, event | category | flops | bytes accessed | tf_op | source)
XLA Modules:
  0.0 358.1 jit_solution(10419687202448267461)
XLA Ops:
  7.3 1.2 constant_dynamic-slice_fusion.1
  8.4 4.9 %collective-permute-start.2 = (bf16[512,512]{1,0:T(8,128)(2,1)S(1)}, bf16[512,512]{1,0:T(8,128)(2,1)S(1)}, u32[]{:S(2)}, u32[]{:S(2)}) collective-permute-start(bf16[512,512]{1,0:T(8,128)(2,1)S(1)} %constant_dynamic-slice_fusion.1), channel_id=1, source_target_pairs={{0,4},{4,8},{8,12},{12,16},{16,20},{20,24},{24,28},{1,5},{5,9},{9,... | collective-permute-start | bytes 1572872 | tf_op jit(solution)/shard_map/ppermute | solution.py:269
  13.3 1.3 collective-permute-start.3
  14.6 21.1 %collective-permute-done.2 = bf16[512,512]{1,0:T(8,128)(2,1)S(1)} collective-permute-done((bf16[512,512]{1,0:T(8,128)(2,1)S(1)}, bf16[512,512]{1,0:T(8,128)(2,1)S(1)}, u32[]{:S(2)}, u32[]{:S(2)}) %collective-permute-start.2) | collective-permute-done | bytes 524320 | tf_op jit(solution)/shard_map/ppermute | solution.py:269
  35.7 1.1 pad_maximum_fusion.2
  36.8 0.2 copy_convert_fusion
  37.1 4.4 %collective-permute-start.4 = (bf16[16,12,128]{2,1,0:T(8,128)(2,1)S(1)}, bf16[16,12,128]{2,1,0:T(8,128)(2,1)S(1)}, u32[]{:S(2)}, u32[]{:S(2)}) collective-permute-start(bf16[16,12,128]{2,1,0:T(8,128)(2,1)S(1)} %constant_dynamic-slice_fusion), channel_id=1, source_target_pairs={{0,4},{4,8},{8,12},{12,16},{16,20},{20,24},{24,28},{1,5},{5,9},{9,... | collective-permute-start | bytes 147464 | tf_op jit(solution)/shard_map/ppermute | solution.py:269
  41.5 1.3 collective-permute-start.5
  42.8 4.9 %collective-permute-start = (s32[64,2]{0,1:T(2,128)S(1)}, s32[64,2]{0,1:T(2,128)S(1)}, u32[]{:S(2)}, u32[]{:S(2)}) collective-permute-start(s32[64,2]{0,1:T(2,128)S(1)} %copy-done.14), channel_id=1, source_target_pairs={{0,4},{4,8},{8,12},{12,16},{16,20},{20,24},{24,28},{1,5},{5,9},{9,... | collective-permute-start | bytes 1544 | tf_op jit(solution)/shard_map/ppermute | solution.py:269
  47.7 1.3 collective-permute-start.1
  49.1 0.1 broadcast_in_dim.9
  49.1 0.1 and.10
  49.2 4.9 %collective-permute-done.1 = s32[64,2]{0,1:T(2,128)S(1)} collective-permute-done((s32[64,2]{0,1:T(2,128)S(1)}, s32[64,2]{0,1:T(2,128)S(1)}, u32[]{:S(2)}, u32[]{:S(2)}) %collective-permute-start.1) | collective-permute-done | bytes 544 | tf_op jit(solution)/shard_map/ppermute | solution.py:269
  54.1 0.1 add_subtract_fusion
  54.2 0.5 fusion.3
  54.7 0.6 broadcast_select_fusion.col_ref
  55.3 10.4 %all-gather.1 = bf16[2,64,12,128]{3,2,1,0:T(8,128)(2,1)S(1)} all-gather(bf16[2,16,12,128]{3,2,1,0:T(8,128)(2,1)S(1)} %pad_maximum_fusion.4), channel_id=3, replica_groups=mesh['gal'=8,'qry'=4] {'qry'}, dimensions={1}, use_global_device_ids=true | all-gather | bytes 491520 | tf_op jit(solution)/shard_map/all_gather | solution.py:285
  65.8 1.0 pad_maximum_fusion.3.near_ref
  66.8 9.6 %all-gather.4.cloned.1.call-done = bf16[2,2048,512]{2,1,0:T(8,128)(2,1)} async-done(((bf16[2,512,512]{2,1,0:T(8,128)(2,1)}), bf16[2,2048,512]{2,1,0:T(8,128)(2,1)}) %all-gather.4.cloned.1.call-update) | async-done | bytes 4194320 | tf_op jit(solution)/shard_map/all_gather | solution.py:285
  76.4 2.6 slice_bitcast_fusion.1
  79.0 0.2 copy-done.7
  79.2 17.6 %pad_maximum_fusion.window_ref = bf16[6144,512]{1,0:T(8,128)(2,1)} fusion(bf16[2048,512]{1,0:T(8,128)(2,1)S(1)} %get-tuple-element.41, bf16[2048,512]{1,0:T(8,128)(2,1)S(1)} %copy-done.7, bf16[2048,512]{1,0:T(8,128)(2,1)S(1)} %get-tuple-element.40), kind=kLoop, calls=%fused_computation.2 | loop fusion | flops 18874368 | bytes 12582912 | tf_op jit(solution)/shard_map/concatenate | solution.py:291
  96.9 39.5 %build_tiles.1 = (bf16[256,128,256]{2,1,0:T(8,128)(2,1)}, f32[2048,128]{1,0:T(8,128)}, s32[256]{0:T(256)}, s32[256]{0:T(256)}, s32[2]{0:T(128)}) custom-call(s32[192]{0:T(256)} %bitcast.25, s32[192]{0:T(256)} %broadcast_select_fusion.col_ref, bf16[6144,512]{1,0:T(8,128)(2,1)} %pad_maximum_fusion.window_ref, bf16[192,12,128]{2,1,0:T(8,128)(2,1)} %pad_maximum_fusion.3.near_ref), custom_call_target="tpu_custom_call" | custom-call | tf_op jit(solution)/shard_map/build_tiles/pallas_call | solution.py:93
  136.4 1.5 add_rsqrt_fusion.refs_4_
  137.9 0.3 slice_reduce_fusion
  138.3 11.5 %collective-permute-start.6 = (f32[2048]{0:T(1024)S(1)}, f32[2048]{0:T(1024)S(1)}, u32[]{:S(2)}, u32[]{:S(2)}) collective-permute-start(f32[2048]{0:T(1024)S(1)} %slice_reduce_fusion), channel_id=1, source_target_pairs={{0,4},{4,8},{8,12},{12,16},{16,20},{20,24},{24,28},{1,5},{5,9},{9,... | collective-permute-start | bytes 24584 | tf_op jit(solution)/shard_map/ppermute | solution.py:269
  149.8 1.3 collective-permute-start.7
  151.1 3.7 %compare_select_fusion = f32[6144,128]{1,0:T(8,128)S(1)} fusion(bf16[128,512]{1,0:T(8,128)(2,1)S(1)} %copy-done, bf16[2048,512]{1,0:T(8,128)(2,1)S(1)} %copy-done.4, bf16[2048,512]{1,0:T(8,128)(2,1)} %param.5, bf16[2048,512]{1,0:T(8,128)(2,1)S(1)} %get-tuple-element.40), kind=kOutput, calls=%fused_computation | convolution fusion | flops 829685760 | bytes 9568256 | tf_op jit(solution)/shard_map/dot_general | solution.py:306
  154.8 0.5 collective-permute-done.7
  155.3 1.5 slice_multiply_fusion.1
  156.8 1.5 pad_maximum_fusion.1.refs_6_.refs_9_
  158.3 12.9 %operator_step.3 = (f32[2048,128]{1,0:T(8,128)}, f32[8,128]{1,0:T(8,128)}, f32[2048,128]{1,0:T(8,128)}) custom-call(s32[256]{0:T(256)} %get-tuple-element.21.refs_0_, s32[256]{0:T(256)} %get-tuple-element.22.refs_1_, s32[2]{0:T(128)} %get-tuple-element.23.refs_2_, bf16[256,128,256]{2,1,0:T(8,128)(2,1)} %get-tuple-element.24.refs_3_, f32[2048,128]{1,0:T(8,128)} %copy-done.2, ...), custom_call_target="tpu_custom_call" | custom-call | tf_op jit(solution)/shard_map/operator_step/pallas_call | solution.py:248
  171.3 5.2 %collective-permute-start.8 = (f32[2048,128]{1,0:T(8,128)}, f32[2048,128]{1,0:T(8,128)S(1)}, u32[]{:S(2)}, u32[]{:S(2)}) collective-permute-start(f32[2048,128]{1,0:T(8,128)} %get-tuple-element.28), channel_id=1, source_target_pairs={{0,4},{4,8},{8,12},{12,16},{16,20},{20,24},{24,28},{1,5},{5,9},{9,... | collective-permute-start | bytes 3145736 | tf_op jit(solution)/shard_map/ppermute | solution.py:269
  176.5 1.3 collective-permute-start.9
  177.8 58.0 %psum.21.refs_5_ = f32[8,128]{1,0:T(8,128)} all-reduce(f32[8,128]{1,0:T(8,128)} %get-tuple-element.26), channel_id=1, replica_groups=mesh['gal'=8,'qry'=4] {'gal'}, use_global_device_ids=true, to_apply=%region_0.1 | all-reduce | flops 1024 | bytes 8192 | tf_op jit(solution)/shard_map/psum | solution.py:315
  235.8 1.0 copy-done.8
  236.8 0.3 copy-done.9
  237.1 16.6 %operator_step.4 = (f32[2048,128]{1,0:T(8,128)}, f32[2048,128]{1,0:T(8,128)}, f32[2048,128]{1,0:T(8,128)}, f32[8,128]{1,0:T(8,128)}, f32[2048,128]{1,0:T(8,128)}...) custom-call(s32[256]{0:T(256)} %get-tuple-element.21.refs_0_, s32[256]{0:T(256)} %get-tuple-element.22.refs_1_, ...), custom_call_target="tpu_custom_call" | custom-call | tf_op jit(solution)/shard_map/operator_step/pallas_call | solution.py:248
  253.7 4.6 %collective-permute-start.10 = (f32[2048,128]{1,0:T(8,128)}, f32[2048,128]{1,0:T(8,128)S(1)}, u32[]{:S(2)}, u32[]{:S(2)}) collective-permute-start(f32[2048,128]{1,0:T(8,128)} %get-tuple-element.35), channel_id=1, source_target_pairs={{0,4},{4,8},{8,12},{12,16},{16,20},{20,24},{24,28},{1,5},{5,9},{9,... | collective-permute-start | bytes 3145736 | tf_op jit(solution)/shard_map/ppermute | solution.py:269
  258.3 1.3 collective-permute-start.11
  259.6 0.8 fusion
  260.4 53.0 %psum.22.refs_5_ = f32[8,128]{1,0:T(8,128)S(1)} all-reduce(f32[8,128]{1,0:T(8,128)} %get-tuple-element.29), channel_id=1, replica_groups=mesh['gal'=8,'qry'=4] {'gal'}, use_global_device_ids=true, to_apply=%region_1.2 | all-reduce | flops 1024 | bytes 8192 | tf_op jit(solution)/shard_map/psum | solution.py:320
  313.4 0.5 copy-done.13
  313.9 0.4 copy-done.10
  314.3 0.3 copy-done.11
  314.7 15.3 %operator_step.5 = (f32[2048,128]{1,0:T(8,128)}, f32[2048,128]{1,0:T(8,128)}, f32[2048,128]{1,0:T(8,128)}, f32[8,128]{1,0:T(8,128)}) custom-call(s32[256]{0:T(256)} %get-tuple-element.21.refs_0_, s32[256]{0:T(256)} %get-tuple-element.22.refs_1_, s32[2]{0:T(128)} %get-tuple-element.23.refs_2_, bf16[256,128,256]{2,1,0:T(8,128)(2,1)} %get-tuple-element.24.refs_3_, ...), custom_call_target="tpu_custom_call" | custom-call | tf_op jit(solution)/shard_map/operator_step/pallas_call | solution.py:248
  330.0 17.4 %psum.23 = f32[8,128]{1,0:T(8,128)S(1)} all-reduce(f32[8,128]{1,0:T(8,128)} %get-tuple-element.36), channel_id=1, replica_groups=mesh['gal'=8,'qry'=4] {'gal'}, use_global_device_ids=true, to_apply=%region_2.3 | all-reduce | flops 1024 | bytes 8192 | tf_op jit(solution)/shard_map/psum | solution.py:324
  347.4 3.8 %multiply_subtract_fusion = (f32[2048,128]{1,0:T(8,128)}, f32[2048,128]{1,0:T(8,128)}) fusion(f32[2048,128]{1,0:T(8,128)} %get-tuple-element.38, f32[2048,128]{1,0:T(8,128)} %get-tuple-element.39, f32[128]{0:T(128)S(1)} %fusion.2, f32[2048,128]{1,0:T(8,128)} %get-tuple-element.37, f32[2048,128]{1,0:T(8,128)S(1)} %copy-done.6, f32[128]{0:T(128)S(1)} %fusion.1, ...), kind=kLoop, calls=%fused_computation.10 | loop fusion | flops 1835008 | bytes 7341568 | tf_op jit(solution)/shard_map/sub | solution.py:327
  (43 shorter events, 0.2 us)
Async XLA Ops:
  7.2 143.9 %copy-start = (bf16[128,512]{1,0:T(8,128)(2,1)S(1)}, bf16[128,512]{1,0:T(8,128)(2,1)}, u32[]{:S(2)}) copy-start(bf16[128,512]{1,0:T(8,128)(2,1)} %param.6) | copy-start | bytes 393220
  7.2 41.9 %copy-start.15 = (s32[3]{0:T(128)S(1)}, s32[3]{0:T(128)}, u32[]{:S(2)}) copy-start(s32[3]{0:T(128)} %constant.37.clone) | copy-start | bytes 40
  7.2 29.6 %copy-start.12 = (s32[64,12,128]{2,0,1:T(8,128)S(1)}, s32[64,12,128]{2,0,1:T(8,128)}, u32[]{:S(2)}) copy-start(s32[64,12,128]{2,0,1:T(8,128)} %param.8) | copy-start | bytes 1179652
  7.2 35.6 %copy-start.14 = (s32[64,2]{0,1:T(2,128)S(1)}, s32[64,2]{0,1:T(2,128)}, u32[]{:S(2)}) copy-start(s32[64,2]{0,1:T(2,128)} %param.7) | copy-start | bytes 1540
  7.2 69.2 %all-gather.4.cloned.1.call-start = ((), (), s32[]{:S(2)}) async-start(), calls=%async_computation | async-start | bytes 5242880 | tf_op jit(solution)/shard_map/all_gather | solution.py:285
  8.4 27.3 %collective-permute-start.2 = (bf16[512,512]{1,0:T(8,128)(2,1)S(1)}, bf16[512,512]{1,0:T(8,128)(2,1)S(1)}, u32[]{:S(2)}, u32[]{:S(2)}) collective-permute-start(bf16[512,512]{1,0:T(8,128)(2,1)S(1)} %constant_dynamic-slice_fusion.1), channel_id=1, source_target_pairs={{0,4},{4,8},{8,12},{12,16},{16,20},{20,24},{24,28},{1,5},{5,9},{9,... | collective-permute-start | bytes 1572872 | tf_op jit(solution)/shard_map/ppermute | solution.py:269
  13.3 22.4 %collective-permute-start.3 = (bf16[512,512]{1,0:T(8,128)(2,1)S(1)}, bf16[512,512]{1,0:T(8,128)(2,1)S(1)}, u32[]{:S(2)}, u32[]{:S(2)}) collective-permute-start(bf16[512,512]{1,0:T(8,128)(2,1)S(1)} %constant_dynamic-slice_fusion.1), channel_id=1, source_target_pairs={{4,0},{8,4},{12,8},{16,12},{20,16},{24,20},{28,24},{5,1},{9,5},{13... | collective-permute-start | bytes 1572872 | tf_op jit(solution)/shard_map/ppermute | solution.py:269
  37.1 18.2 %collective-permute-start.4 = (bf16[16,12,128]{2,1,0:T(8,128)(2,1)S(1)}, bf16[16,12,128]{2,1,0:T(8,128)(2,1)S(1)}, u32[]{:S(2)}, u32[]{:S(2)}) collective-permute-start(bf16[16,12,128]{2,1,0:T(8,128)(2,1)S(1)} %constant_dynamic-slice_fusion), channel_id=1, source_target_pairs={{0,4},{4,8},{8,12},{12,16},{16,20},{20,24},{24,28},{1,5},{5,9},{9,... | collective-permute-start | bytes 147464 | tf_op jit(solution)/shard_map/ppermute | solution.py:269
  41.5 13.8 %collective-permute-start.5 = (bf16[16,12,128]{2,1,0:T(8,128)(2,1)S(1)}, bf16[16,12,128]{2,1,0:T(8,128)(2,1)S(1)}, u32[]{:S(2)}, u32[]{:S(2)}) collective-permute-start(bf16[16,12,128]{2,1,0:T(8,128)(2,1)S(1)} %constant_dynamic-slice_fusion), channel_id=1, source_target_pairs={{4,0},{8,4},{12,8},{16,12},{20,16},{24,20},{28,24},{5,1},{9,5},{13... | collective-permute-start | bytes 147464 | tf_op jit(solution)/shard_map/ppermute | solution.py:269
  42.8 6.5 %collective-permute-start = (s32[64,2]{0,1:T(2,128)S(1)}, s32[64,2]{0,1:T(2,128)S(1)}, u32[]{:S(2)}, u32[]{:S(2)}) collective-permute-start(s32[64,2]{0,1:T(2,128)S(1)} %copy-done.14), channel_id=1, source_target_pairs={{0,4},{4,8},{8,12},{12,16},{16,20},{20,24},{24,28},{1,5},{5,9},{9,... | collective-permute-start | bytes 1544 | tf_op jit(solution)/shard_map/ppermute | solution.py:269
  47.7 6.4 %collective-permute-start.1 = (s32[64,2]{0,1:T(2,128)S(1)}, s32[64,2]{0,1:T(2,128)S(1)}, u32[]{:S(2)}, u32[]{:S(2)}) collective-permute-start(s32[64,2]{0,1:T(2,128)S(1)} %copy-done.14), channel_id=1, source_target_pairs={{4,0},{8,4},{12,8},{16,12},{20,16},{24,20},{28,24},{5,1},{9,5},{13... | collective-permute-start | bytes 1544 | tf_op jit(solution)/shard_map/ppermute | solution.py:269
  76.4 2.9 copy-start.7
  79.0 17.8 %copy-start.3 = (bf16[2048,512]{1,0:T(8,128)(2,1)}, bf16[2048,512]{1,0:T(8,128)(2,1)S(1)}, u32[]{:S(2)}) copy-start(bf16[2048,512]{1,0:T(8,128)(2,1)S(1)} %get-tuple-element.41) | copy-start | bytes 6291460
  136.4 14.7 %copy-start.4 = (bf16[2048,512]{1,0:T(8,128)(2,1)S(1)}, bf16[2048,512]{1,0:T(8,128)(2,1)}, u32[]{:S(2)}) copy-start(bf16[2048,512]{1,0:T(8,128)(2,1)} %copy-done.3) | copy-start | bytes 6291460
  137.9 16.8 %copy-start.2 = (f32[2048,128]{1,0:T(8,128)}, f32[2048,128]{1,0:T(8,128)S(1)}, u32[]{:S(2)}) copy-start(f32[2048,128]{1,0:T(8,128)S(1)} %add_rsqrt_fusion.refs_4_) | copy-start | bytes 3145732
  138.3 16.5 %collective-permute-start.6 = (f32[2048]{0:T(1024)S(1)}, f32[2048]{0:T(1024)S(1)}, u32[]{:S(2)}, u32[]{:S(2)}) collective-permute-start(f32[2048]{0:T(1024)S(1)} %slice_reduce_fusion), channel_id=1, source_target_pairs={{0,4},{4,8},{8,12},{12,16},{16,20},{20,24},{24,28},{1,5},{5,9},{9,... | collective-permute-start | bytes 24584 | tf_op jit(solution)/shard_map/ppermute | solution.py:269
  149.8 5.5 %collective-permute-start.7 = (f32[2048]{0:T(1024)S(1)}, f32[2048]{0:T(1024)S(1)}, u32[]{:S(2)}, u32[]{:S(2)}) collective-permute-start(f32[2048]{0:T(1024)S(1)} %slice_reduce_fusion), channel_id=1, source_target_pairs={{4,0},{8,4},{12,8},{16,12},{20,16},{24,20},{28,24},{5,1},{9,5},{13... | collective-permute-start | bytes 24584 | tf_op jit(solution)/shard_map/ppermute | solution.py:269
  154.8 2.0 copy-start.5
  171.3 64.5 %collective-permute-start.8 = (f32[2048,128]{1,0:T(8,128)}, f32[2048,128]{1,0:T(8,128)S(1)}, u32[]{:S(2)}, u32[]{:S(2)}) collective-permute-start(f32[2048,128]{1,0:T(8,128)} %get-tuple-element.28), channel_id=1, source_target_pairs={{0,4},{4,8},{8,12},{12,16},{16,20},{20,24},{24,28},{1,5},{5,9},{9,... | collective-permute-start | bytes 3145736 | tf_op jit(solution)/shard_map/ppermute | solution.py:269
  176.5 59.3 %collective-permute-start.9 = (f32[2048,128]{1,0:T(8,128)}, f32[2048,128]{1,0:T(8,128)S(1)}, u32[]{:S(2)}, u32[]{:S(2)}) collective-permute-start(f32[2048,128]{1,0:T(8,128)} %get-tuple-element.28), channel_id=1, source_target_pairs={{4,0},{8,4},{12,8},{16,12},{20,16},{24,20},{28,24},{5,1},{9,5},{13... | collective-permute-start | bytes 3145736 | tf_op jit(solution)/shard_map/ppermute | solution.py:269
  235.8 1.0 copy-start.8
  235.8 1.3 copy-start.9
  253.7 59.7 %collective-permute-start.10 = (f32[2048,128]{1,0:T(8,128)}, f32[2048,128]{1,0:T(8,128)S(1)}, u32[]{:S(2)}, u32[]{:S(2)}) collective-permute-start(f32[2048,128]{1,0:T(8,128)} %get-tuple-element.35), channel_id=1, source_target_pairs={{0,4},{4,8},{8,12},{12,16},{16,20},{20,24},{24,28},{1,5},{5,9},{9,... | collective-permute-start | bytes 3145736 | tf_op jit(solution)/shard_map/ppermute | solution.py:269
  258.3 55.1 %collective-permute-start.11 = (f32[2048,128]{1,0:T(8,128)}, f32[2048,128]{1,0:T(8,128)S(1)}, u32[]{:S(2)}, u32[]{:S(2)}) collective-permute-start(f32[2048,128]{1,0:T(8,128)} %get-tuple-element.35), channel_id=1, source_target_pairs={{4,0},{8,4},{12,8},{16,12},{20,16},{24,20},{28,24},{5,1},{9,5},{13... | collective-permute-start | bytes 3145736 | tf_op jit(solution)/shard_map/ppermute | solution.py:269
  313.3 0.6 copy-start.13
  313.4 1.0 copy-start.10
  313.4 1.3 copy-start.11
  314.7 32.7 %copy-start.6 = (f32[2048,128]{1,0:T(8,128)S(1)}, f32[2048,128]{1,0:T(8,128)}, u32[]{:S(2)}) copy-start(f32[2048,128]{1,0:T(8,128)} %get-tuple-element.30.refs_7_) | copy-start | bytes 3145732
  347.4 3.9 %copy-start.1 = (bf16[128,512]{1,0:T(8,128)(2,1)S(1)}, bf16[128,512]{1,0:T(8,128)(2,1)}, u32[]{:S(2)}) copy-start(bf16[128,512]{1,0:T(8,128)(2,1)} %param.6) | copy-start | bytes 393220
Sparse Core Ops, SparseCore 0:
  36.9 39.4 all-gather.3

commit v2 on v1

--- a/solution.py
+++ b/solution.py
@@ -84,8 +84,8 @@
         pltpu.make_async_copy(stage.at[place], mats_ref.at[0], sems.at[place]).wait()
 
 
-def build(row, col, window, near):
-    total, entries, _ = near.shape
+def build(entries, row, col, window, near):
+    total = near.shape[0]
     tiles = total // 3
     blocks = window.shape[0] // (3 * BLK)
     smem = pl.BlockSpec(memory_space=pltpu.SMEM)
@@ -262,11 +262,231 @@
     )(dst, src, count, mats, scale, *rest)
 
 
-def from_sides(value):
+def peer(axis, index):
+    return {axis: index}
+
+
+def signal_all(others):
+    barrier = pltpu.get_barrier_semaphore()
+    for exists, axis, index in others:
+        def hello(axis=axis, index=index):
+            pl.semaphore_signal(barrier, inc=1, device_id=peer(axis, index),
+                                device_id_type=pl.DeviceIdType.MESH)
+
+        if exists is None:
+            hello()
+        else:
+            pl.when(exists)(hello)
+    always = sum(exists is None for exists, _, _ in others)
+    perhaps = [exists.astype(jnp.int32) for exists, _, _ in others if exists is not None]
+    pl.semaphore_wait(barrier, functools.reduce(lambda x, y: x + y, perhaps, always))
+
+
+def remote(src, dst, send, recv, axis, index):
+    return pltpu.make_async_remote_copy(
+        src_ref=src, dst_ref=dst, send_sem=send, recv_sem=recv,
+        device_id=peer(axis, index), device_id_type=pl.DeviceIdType.MESH,
+    )
+
+
+def sides_of(count):
+    me = lax.axis_index("gal")
+    up = lax.rem(me + 1, count)
+    down = lax.rem(me + count - 1, count)
+    return me, ((me + 1 < count, up), (me > 0, down))
+
+
+def swap_kernel(count, with_field, with_sums, *refs):
+    refs = list(refs)
+    field = refs.pop(0) if with_field else None
+    sums = refs.pop(0) if with_sums else None
+    outs = (refs.pop(0), refs.pop(0)) if with_field else None
+    sums_out = refs.pop(0) if with_sums else None
+    me, sides = sides_of(count)
+    if with_sums:
+        slots, sum_send, sum_recv = refs[:3]
+        refs = refs[3:]
+        signal_all([(None, "gal", lax.rem(me + o, count)) for o in range(1, count)])
+    else:
+        signal_all([(exists, "gal", index) for exists, index in sides])
+    if with_sums:
+        sends = [
+            remote(sums, slots.at[o], sum_send.at[o], sum_recv.at[o], "gal", lax.rem(me + o, count))
+            for o in range(1, count)
+        ]
+        for copy in sends:
+            copy.start()
+    if with_field:
+        send, recv = refs
+        copies = [
+            remote(field, outs[i], send.at[i], recv.at[i], "gal", index)
+            for i, (_, index) in enumerate(sides)
+        ]
+        for copy, (exists, _) in zip(copies, sides):
+            pl.when(exists)(copy.start)
+    if with_sums:
+        for copy in sends:
+            copy.wait()
+        all_sums = sums[...]
+        for o in range(1, count):
+            all_sums += slots[o]
+        sums_out[...] = all_sums
+    if with_field:
+        for i in range(2):
+            pl.when(sides[i][0])(copies[i].wait_send)
+            pl.when(sides[1 - i][0])(copies[i].wait_recv)
+
+
+def swap(ident, field=None, sums=None):
     count = lax.axis_size("gal")
-    up = [(i, i + 1) for i in range(count - 1)]
-    down = [(i + 1, i) for i in range(count - 1)]
-    return lax.ppermute(value, "gal", up), lax.ppermute(value, "gal", down)
+    anywhere = pl.BlockSpec(memory_space=pl.ANY)
+    vmem = pl.BlockSpec(memory_space=pltpu.VMEM)
+    args, specs, outs, out_specs, scratch = [], [], [], [], []
+    if field is not None:
+        args.append(field)
+        specs.append(anywhere)
+        outs += [jax.ShapeDtypeStruct(field.shape, field.dtype)] * 2
+        out_specs += [anywhere] * 2
+    if sums is not None:
+        args.append(sums)
+        specs.append(vmem)
+        outs.append(jax.ShapeDtypeStruct(sums.shape, sums.dtype))
+        out_specs.append(vmem)
+        scratch += [
+            pltpu.VMEM((count,) + sums.shape, sums.dtype),
+            pltpu.SemaphoreType.DMA((count,)),
+            pltpu.SemaphoreType.DMA((count,)),
+        ]
+    if field is not None:
+        scratch += [pltpu.SemaphoreType.DMA((2,)), pltpu.SemaphoreType.DMA((2,))]
+    return pl.pallas_call(
+        functools.partial(swap_kernel, count, field is not None, sums is not None),
+        out_shape=tuple(outs),
+        in_specs=specs,
+        out_specs=tuple(out_specs),
+        scratch_shapes=scratch,
+        compiler_params=pltpu.CompilerParams(collective_id=ident, has_side_effects=True),
+        name="swap",
+    )(*args)
+
+
+PIECES = 2
+
+
+def gather_kernel(count, parts, own, near, window, near_all,
+                  far_send, far_recv, local_sems, *level_sems):
+    rows, tiles = own.shape[0], near.shape[0]
+    size, tile_size = rows // parts, tiles // parts
+    step, tile_step = size // PIECES, tile_size // PIECES
+    part = lax.axis_index("qry")
+    me, sides = sides_of(count)
+    bits = [1 << b for b in reversed(range(parts.bit_length() - 1))]
+
+    def partner(bit):
+        return part + bit - 2 * bit * lax.rem(part // bit, 2)
+
+    signal_all([(exists, "gal", index) for exists, index in sides]
+               + [(None, "qry", partner(bit)) for bit in bits])
+    locals_ = [
+        pltpu.make_async_copy(own, window.at[pl.ds(rows, rows)], local_sems.at[0]),
+        pltpu.make_async_copy(near, near_all.at[pl.ds(0, tiles)], local_sems.at[1]),
+    ]
+
+    def pair(index, piece, side):
+        at = index * size + piece * step
+        near_at = index * tile_size + piece * tile_step
+        base = (0, 2 * rows)[side]
+        near_base = (tiles, 2 * tiles)[side]
+        return (
+            (own.at[pl.ds(at, step)], window.at[pl.ds(base + at, step)]),
+            (near.at[pl.ds(near_at, tile_step)], near_all.at[pl.ds(near_base + near_at, tile_step)]),
+        )
+
+    far = {}
+    for piece in range(PIECES):
+        for i, (_, index) in enumerate(sides):
+            far[piece, i] = [
+                remote(src, dst, far_send.at[piece, i, k], far_recv.at[piece, i, k], "gal", index)
+                for k, (src, dst) in enumerate(pair(part, piece, i))
+            ]
+    for piece in range(PIECES):
+        for i, (exists, _) in enumerate(sides):
+            for copy in far[piece, i]:
+                pl.when(exists)(copy.start)
+    for copy in locals_:
+        copy.start()
+
+    def forward(piece, side, level):
+        bit = bits[level]
+        held = [part]
+        for earlier in bits[:level]:
+            held = held + [index + (partner(earlier) - part) for index in held]
+        send, recv = level_sems[2 * level:2 * level + 2]
+        return [
+            remote(spot, spot, send.at[piece, side, n, k], recv.at[piece, side, n, k],
+                   "qry", partner(bit))
+            for n, index in enumerate(held)
+            for k, (_, spot) in enumerate(pair(index, piece, side))
+        ]
+
+    order = [(piece, side) for piece in range(PIECES) for side in range(2)]
+    for piece, side in order:
+        @pl.when(sides[1 - side][0])
+        def _(piece=piece, side=side):
+            for copy in far[piece, side]:
+                copy.wait_recv()
+            for copy in forward(piece, side, 0):
+                copy.start()
+
+    for level in range(1, len(bits)):
+        for piece, side in order:
+            @pl.when(sides[1 - side][0])
+            def _(piece=piece, side=side, level=level):
+                for copy in forward(piece, side, level - 1):
+                    copy.wait_recv()
+                for copy in forward(piece, side, level):
+                    copy.start()
+
+    for piece, side in order:
+        @pl.when(sides[1 - side][0])
+        def _(piece=piece, side=side):
+            for copy in forward(piece, side, len(bits) - 1):
+                copy.wait_recv()
+            for level in range(len(bits)):
+                for copy in forward(piece, side, level):
+                    copy.wait_send()
+
+        @pl.when(sides[side][0])
+        def _(piece=piece, side=side):
+            for copy in far[piece, side]:
+                copy.wait_send()
+
+    for copy in locals_:
+        copy.wait()
+
+
+def gather(own, near):
+    count, parts = lax.axis_size("gal"), lax.axis_size("qry")
+    anywhere = pl.BlockSpec(memory_space=pl.ANY)
+    levels = []
+    for level in range(parts.bit_length() - 1):
+        levels += [pltpu.SemaphoreType.DMA((PIECES, 2, 1 << level, 2))] * 2
+    return pl.pallas_call(
+        functools.partial(gather_kernel, count, parts),
+        out_shape=(
+            jax.ShapeDtypeStruct((3 * own.shape[0],) + own.shape[1:], own.dtype),
+            jax.ShapeDtypeStruct((3 * near.shape[0],) + near.shape[1:], near.dtype),
+        ),
+        in_specs=[anywhere] * 2,
+        out_specs=(anywhere, anywhere),
+        scratch_shapes=[
+            pltpu.SemaphoreType.DMA((PIECES, 2, 2)),
+            pltpu.SemaphoreType.DMA((PIECES, 2, 2)),
+            pltpu.SemaphoreType.DMA((2,)),
+        ] + levels,
+        compiler_params=pltpu.CompilerParams(collective_id=0, has_side_effects=True),
+        name="gather_beside",
+    )(own, near)
 
 
 def per_device(descriptors, query_descriptors, tile_blocks, neighbours):
@@ -275,53 +495,43 @@
     blocks = rows // BLK
     place = lax.axis_index("gal")
     count = lax.axis_size("gal")
-    parts = lax.axis_size("qry")
-    part = lax.axis_index("qry")
-
-    def spread(value):
-        size = value.shape[0] // parts
-        piece = lax.dynamic_slice_in_dim(value, part * size, size, axis=0)
-        pieces = jnp.stack(from_sides(piece))
-        whole = lax.all_gather(pieces, "qry", axis=1)
-        return whole.reshape((2,) + value.shape)
-
-    near = neighbours.astype(jnp.bfloat16)
-    beside = spread(descriptors)
-    near_beside = spread(near)
-    window = jnp.concatenate([beside[0], descriptors, beside[1]], axis=0)
-    near_all = jnp.concatenate([near, near_beside[0], near_beside[1]], axis=0)
-    below, above = from_sides(tile_blocks)
-    base = (place - 1) * blocks
-    far = jnp.int32(3 * blocks)
-    local = jnp.concatenate([tile_blocks, below, above], axis=0) - base
-    origin = jnp.repeat(jnp.array([0, -1, 1], jnp.int32), tiles) + place
+    entries = neighbours.shape[1]
+
+    first = place * blocks
+    spot = tile_blocks - jnp.stack([first, first - blocks])[None, :]
+    spots = jnp.pad(spot, ((0, 0), (0, BLK - 2)))[:, None, :]
+    near = jnp.concatenate([neighbours, spots], axis=1)
+    near = jnp.pad(near, ((0, 0), (0, 16 - entries - 1), (0, 0))).astype(jnp.bfloat16)
+    window, near_all = gather(descriptors, near)
+    spots = near_all[:, entries, 0:2].astype(jnp.int32)
+    shift = jnp.repeat(jnp.array([0, -1, 1], jnp.int32), tiles)
+    origin = shift + place
     exists = jnp.logical_and(origin >= 0, origin < count)
-    row = local[:, 0]
-    col = jnp.where(exists, local[:, 1], far)
-
-    mats, degree, dst, src, used = build(row, col, window, near_all)
+    row = spots[:, 0] + (1 + shift) * blocks
+    col = jnp.where(exists, spots[:, 1] + shift * blocks, jnp.int32(3 * blocks))
+
+    mats, degree, dst, src, used = build(entries, row, col, window, near_all)
     scale = 1.0 / jnp.sqrt(1.0 + degree)
-    scale_low, scale_high = from_sides(scale[:, 0])
+    scale_low, scale_high = swap(1, scale[:, 0].reshape(blocks, BLK))
     seeds = jax.nn.softplus(
         lax.dot_general(window, query_descriptors, (((1,), (1,)), ((), ())),
                         preferred_element_type=jnp.float32) / math.sqrt(width)
     )
     own = seeds[rows:2 * rows]
     halo = jnp.concatenate(
-        [seeds[:rows] * scale_low[:, None], seeds[2 * rows:] * scale_high[:, None]], axis=0
+        [seeds[:rows] * scale_low.reshape(rows, 1), seeds[2 * rows:] * scale_high.reshape(rows, 1)],
+        axis=0,
     )
     image0, sums0, send0 = run_step(0, dst, src, used, mats, scale, own, halo)
-    fresh = from_sides(send0)
-    sums0 = lax.psum(sums0, "gal")
+    low0, high0, sums0 = swap(2, send0, sums0)
     res1, dir1, image1, sums1, send1, halo1, tail1 = run_step(
-        1, dst, src, used, mats, scale, sums0, own, own, image0, halo, *fresh
+        1, dst, src, used, mats, scale, sums0, own, own, image0, halo, low0, high0
     )
-    fresh = from_sides(send1)
-    sums1 = lax.psum(sums1, "gal")
+    low1, high1, sums1 = swap(2, send1, sums1)
     res2, dir2, image2, sums2 = run_step(
-        2, dst, src, used, mats, scale, sums1, res1, dir1, image1, halo1, tail1, *fresh
+        2, dst, src, used, mats, scale, sums1, res1, dir1, image1, halo1, tail1, low1, high1
     )
-    sums2 = lax.psum(sums2, "gal")
+    (sums2,) = swap(3, None, sums2)
     alpha0, alpha1, alpha2 = (s[0:1] / s[1:2] for s in (sums0, sums1, sums2))
     ranking = alpha0 * own + alpha1 * dir1 + alpha2 * dir2
     residual = res2 - alpha2 * image2

time: 361 us -> 315 us (0.87); the launches traced: 358 us -> 316 us
  Pallas kernels: 84.3 us -> 289 us
  blocking collectives: 139 us -> 0 us
  starting transfers between devices: 43.4 us -> 0 us
  waiting for transfers between devices: 36.1 us -> 0 us
  between operations: 14.4 us -> 0.77 us
  other arithmetic: 29.7 us -> 16.6 us
  local copies, waits for them, and re-layouts: 7.74 us -> 3.24 us
    pallas_call x0 -> x5, Pallas kernels: none -> 208 us  [the longest x4 132 us: swap(): pl.pallas_call(functools.partial(swap_kernel, count, field is not None, s...]
    psum x3 -> x0, blocking collectives: 128 us -> none  [the longest x1 58 us: per_device(): sums0 = lax.psum(sums0, 'gal')]
    ppermute x12 -> x0, starting transfers between devices: 43.3 us -> none  [from_sides(): return (lax.ppermute(value, 'gal', up), lax.ppermute(value, 'gal', down))]
    ppermute x12 -> x0, waiting for transfers between devices: 26.5 us -> none  [from_sides(): return (lax.ppermute(value, 'gal', up), lax.ppermute(value, 'gal', down))]
    concatenate x3 -> x2, other arithmetic: 20.2 us -> 2.27 us  [the longest x1 1.45 us: per_device(): jnp.concatenate([seeds[:rows] * scale_low.reshape(rows, 1), seeds[2 * row...]
    all_gather x1 -> x0, blocking collectives: 10.4 us -> none  [spread(): whole = lax.all_gather(pieces, 'qry', axis=1)]
    all_gather x1 -> x0, waiting for transfers between devices: 9.57 us -> none  [spread(): whole = lax.all_gather(pieces, 'qry', axis=1)]
  transfers between devices with their start and end apart: 13 -> 0, of which waited for: 4 -> 0; matrix products, arithmetic and copies ran while one was open for 2% -> 0% of each run, Pallas kernels for 0% -> 0%
where the time goes in v2:
time: 315 us; the launch traced here: 316 us
  Pallas kernels  289 us (92%)
  other arithmetic  16.6 us (5%)
  matrix products  6.55 us (2%)
  local copies, waits for them, and re-layouts  3.24 us (1%)
    pallas_call x4, Pallas kernels, swap(): pl.pallas_call(functools.partial(swap_kernel, count, field is not None, s...  132 us
    pallas_call x1, Pallas kernels, gather(): pl.pallas_call(functools.partial(gather_kernel, count, parts), out_shape=...  76.1 us
    pallas_call x3, Pallas kernels, run_step(): pl.pallas_call(functools.partial(step_kernel, step, blocks, tiles), out_s...  41.9 us
    pallas_call x1, Pallas kernels, build(): pl.pallas_call(functools.partial(build_kernel, tiles, entries, blocks), o...  38.2 us
    dot_general x1, matrix products, per_device(): lax.dot_general(window, query_descriptors, (((1,), (1,)), ((), ())), pref...  6.55 us

profile of v2, /device:TPU:0, one launch (start us, length us, event | category | flops | bytes accessed | tf_op | source)
XLA Modules:
  0.0 315.7 jit_solution(1653802870736751524)
XLA Ops:
  0.6 0.0 copy-start
  0.7 0.1 pad_add_fusion
  0.7 0.8 subtract_convert_fusion
  1.5 0.7 compare_and_fusion
  2.1 0.1 broadcast_in_dim.18
  2.2 0.1 and.9
  2.3 0.7 broadcast_in_dim.17
  3.0 0.1 mul.75
  3.1 0.7 broadcast_in_dim.19
  3.8 0.1 mul.77
  3.9 0.1 copy.16
  4.0 1.0 convert.12
  5.1 0.1 copy.15
  5.2 0.8 fusion.2.near
  6.0 76.1 %gather_beside.1 = (bf16[6144,512]{1,0:T(8,128)(2,1)}, bf16[192,16,128]{2,1,0:T(8,128)(2,1)}) custom-call(bf16[2048,512]{1,0:T(8,128)(2,1)} %own.1, bf16[64,16,128]{2,1,0:T(8,128)(2,1)} %fusion.2.near), custom_call_target="tpu_custom_call" | custom-call | tf_op jit(solution)/shard_map/gather_beside/pallas_call | solution.py:474
  82.2 1.2 slice_convert_fusion
  83.3 0.2 slice_reduce_fusion.1
  83.6 0.5 add_select_fusion.col_ref
  84.1 0.6 add.42.row_ref
  84.7 0.0 copy-done
  84.7 6.5 %compare_select_fusion = f32[6144,128]{1,0:T(8,128)} fusion(bf16[6144,512]{1,0:T(8,128)(2,1)} %get-tuple-element.32.window_ref, bf16[128,512]{1,0:T(8,128)(2,1)S(1)} %copy-done), kind=kOutput, calls=%fused_computation | convolution fusion | flops 810811392 | bytes 9568256 | tf_op jit(solution)/shard_map/dot_general | solution.py:517
  91.2 38.2 %build_tiles.1 = (bf16[256,128,256]{2,1,0:T(8,128)(2,1)}, f32[2048,128]{1,0:T(8,128)}, s32[256]{0:T(256)}, s32[256]{0:T(256)}, s32[2]{0:T(128)}) custom-call(s32[192]{0:T(256)} %add.42.row_ref, s32[192]{0:T(256)} %add_select_fusion.col_ref, bf16[6144,512]{1,0:T(8,128)(2,1)} %get-tuple-element.32.window_ref, bf16[192,16,128]{2,1,0:T(8,128)(2,1)} %get-tuple-element.31.near_ref), custom_call_target="tpu_custom_call" | custom-call | tf_op jit(solution)/shard_map/build_tiles/pallas_call | solution.py:93
  129.4 1.4 add_rsqrt_fusion.refs_4_
  130.8 0.0 copy-start.1
  130.8 1.0 slice_reduce_fusion
  131.8 17.0 %swap.4 = (f32[16,128]{1,0:T(8,128)}, f32[16,128]{1,0:T(8,128)}) custom-call(f32[16,128]{1,0:T(8,128)} %bitcast.17), custom_call_target="tpu_custom_call" | custom-call | tf_op jit(solution)/shard_map/swap/pallas_call | solution.py:362
  148.7 3.0 slice_multiply_fusion.1
  151.7 0.0 copy-done.1
  151.7 1.4 pad_maximum_fusion.refs_6_.refs_9_
  153.1 12.1 %operator_step.3 = (f32[2048,128]{1,0:T(8,128)}, f32[8,128]{1,0:T(8,128)}, f32[2048,128]{1,0:T(8,128)}) custom-call(s32[256]{0:T(256)} %get-tuple-element.33.refs_0_, s32[256]{0:T(256)} %get-tuple-element.34.refs_1_, s32[2]{0:T(128)} %get-tuple-element.35.refs_2_, bf16[256,128,256]{2,1,0:T(8,128)(2,1)} %get-tuple-element.36.refs_3_, f32[2048,128]{1,0:T(8,128)} %copy-done.1, ...), custom_call_target="tpu_custom_call" | custom-call | tf_op jit(solution)/shard_map/operator_step/pallas_call | solution.py:248
  165.2 51.2 %swap.5 = (f32[2048,128]{1,0:T(8,128)}, f32[2048,128]{1,0:T(8,128)}, f32[8,128]{1,0:T(8,128)}) custom-call(f32[2048,128]{1,0:T(8,128)} %get-tuple-element.40.refs_0_, f32[8,128]{1,0:T(8,128)} %get-tuple-element.41.refs_1_), custom_call_target="tpu_custom_call" | custom-call | tf_op jit(solution)/shard_map/swap/pallas_call | solution.py:362
  216.4 15.5 %operator_step.4 = (f32[2048,128]{1,0:T(8,128)}, f32[2048,128]{1,0:T(8,128)}, f32[2048,128]{1,0:T(8,128)}, f32[8,128]{1,0:T(8,128)}, f32[2048,128]{1,0:T(8,128)}...) custom-call(s32[256]{0:T(256)} %get-tuple-element.33.refs_0_, s32[256]{0:T(256)} %get-tuple-element.34.refs_1_, ...), custom_call_target="tpu_custom_call" | custom-call | tf_op jit(solution)/shard_map/operator_step/pallas_call | solution.py:248
  231.9 52.7 %swap.6 = (f32[2048,128]{1,0:T(8,128)}, f32[2048,128]{1,0:T(8,128)}, f32[8,128]{1,0:T(8,128)}) custom-call(f32[2048,128]{1,0:T(8,128)} %get-tuple-element.46.refs_0_, f32[8,128]{1,0:T(8,128)} %get-tuple-element.47.refs_1_), custom_call_target="tpu_custom_call" | custom-call | tf_op jit(solution)/shard_map/swap/pallas_call | solution.py:362
  284.6 0.8 fusion.3
  285.4 0.0 copy-start.2
  285.4 14.4 %operator_step.5 = (f32[2048,128]{1,0:T(8,128)}, f32[2048,128]{1,0:T(8,128)}, f32[2048,128]{1,0:T(8,128)}, f32[8,128]{1,0:T(8,128)}) custom-call(s32[256]{0:T(256)} %get-tuple-element.33.refs_0_, s32[256]{0:T(256)} %get-tuple-element.34.refs_1_, s32[2]{0:T(128)} %get-tuple-element.35.refs_2_, bf16[256,128,256]{2,1,0:T(8,128)(2,1)} %get-tuple-element.36.refs_3_, ...), custom_call_target="tpu_custom_call" | custom-call | tf_op jit(solution)/shard_map/operator_step/pallas_call | solution.py:248
  299.8 11.5 %swap.7 = f32[8,128]{1,0:T(8,128)} custom-call(f32[8,128]{1,0:T(8,128)} %get-tuple-element.56.refs_0_), custom_call_target="tpu_custom_call" | custom-call | tf_op jit(solution)/shard_map/swap/pallas_call | solution.py:362
  311.2 0.8 fusion.5
  312.0 0.0 copy-done.2
  312.0 3.7 %multiply_subtract_fusion = (f32[2048,128]{1,0:T(8,128)}, f32[2048,128]{1,0:T(8,128)}) fusion(f32[2048,128]{1,0:T(8,128)} %get-tuple-element.58, f32[2048,128]{1,0:T(8,128)} %get-tuple-element.59, f32[128]{0:T(128)S(1)} %fusion.5, f32[2048,128]{1,0:T(8,128)} %get-tuple-element.57, f32[2048,128]{1,0:T(8,128)S(1)} %copy-done.2, f32[128]{0:T(128)S(1)} %get-tuple-element.68, ...), kind=kLoop, calls=%fused_computation.6 | loop fusion | flops 1835008 | bytes 7341568 | tf_op jit(solution)/shard_map/sub | solution.py:537
  (1 shorter events, 0.0 us)
Async XLA Ops:
  0.6 84.0 %copy-start = (bf16[128,512]{1,0:T(8,128)(2,1)S(1)}, bf16[128,512]{1,0:T(8,128)(2,1)}, u32[]{:S(2)}) copy-start(bf16[128,512]{1,0:T(8,128)(2,1)} %param.6) | copy-start | bytes 393220
  130.8 20.9 %copy-start.1 = (f32[2048,128]{1,0:T(8,128)}, f32[2048,128]{1,0:T(8,128)S(1)}, u32[]{:S(2)}) copy-start(f32[2048,128]{1,0:T(8,128)S(1)} %add_rsqrt_fusion.refs_4_) | copy-start | bytes 3145732
  285.4 26.6 %copy-start.2 = (f32[2048,128]{1,0:T(8,128)S(1)}, f32[2048,128]{1,0:T(8,128)}, u32[]{:S(2)}) copy-start(f32[2048,128]{1,0:T(8,128)} %get-tuple-element.49.refs_7_) | copy-start | bytes 3145732

commit v3 on v2

--- a/solution.py
+++ b/solution.py
@@ -10,22 +10,25 @@
 
 BLK = 128
 DAMPING = 0.99
-STAGE = 4
+STAGE = 8
+GROUP = 2
 CHUNK = 16
 VMEM_LIMIT = 60 * 1024 * 1024
 
 
 def softplus(value):
-    return jnp.maximum(value, 0.0) + jnp.log1p(jnp.exp(-jnp.abs(value)))
+    return jnp.maximum(value, 0.0) + jnp.log(1.0 + jnp.exp(-jnp.abs(value)))
 
 
 def build_kernel(tiles, entries, blocks, row_ref, col_ref, window_ref, near_ref,
-                 mats_ref, degree_ref, dst_ref, src_ref, count_ref, stage, sems):
+                 mats_ref, degree_ref, dst_ref, src_ref, count_ref, stage, listed, sems):
     root = 1.0 / math.sqrt(window_ref.shape[1])
     degree_ref[...] = jnp.zeros_like(degree_ref)
     count_ref[0] = 0
     count_ref[1] = 0
-    places = lax.broadcasted_iota(jnp.int32, (BLK, BLK), 0).astype(jnp.float32)
+    places = lax.broadcasted_iota(jnp.int32, (BLK, BLK), 0).astype(jnp.float32).astype(jnp.bfloat16)
+    ones = jnp.ones((2 * BLK, BLK), jnp.bfloat16)
+    one, none = jnp.bfloat16(1.0), jnp.bfloat16(0.0)
 
     def emit(mat, slot, dst, src):
         sent = count_ref[0]
@@ -36,25 +39,25 @@
             pltpu.make_async_copy(stage.at[place], mats_ref.at[0], sems.at[place]).wait()
 
         high = mat.astype(jnp.bfloat16)
-        stage[place, :, 0:BLK] = high
-        stage[place, :, BLK:] = (mat - high.astype(jnp.float32)).astype(jnp.bfloat16)
+        both = jnp.concatenate([high, (mat - high.astype(jnp.float32)).astype(jnp.bfloat16)], axis=1)
+        stage[place] = both
         pltpu.make_async_copy(stage.at[place], mats_ref.at[slot], sems.at[place]).start()
         count_ref[0] = sent + 1
         dst_ref[slot] = dst
         src_ref[slot] = src
         rows = pl.ds(pl.multiple_of(dst * BLK, BLK), BLK)
-        degree_ref[rows, :] += jnp.broadcast_to(jnp.sum(mat, axis=1, keepdims=True), (BLK, BLK))
+        degree_ref[rows, :] += jnp.dot(both, ones, preferred_element_type=jnp.float32)
 
     def turned(t):
         left = window_ref[pl.ds(pl.multiple_of(row_ref[t] * BLK, BLK), BLK), :]
         right = window_ref[pl.ds(pl.multiple_of(col_ref[t] * BLK, BLK), BLK), :]
         dots = lax.dot_general(right, left, (((1,), (1,)), ((), ())),
                                preferred_element_type=jnp.float32)
-        near = near_ref[t].astype(jnp.float32)
-        counted = jnp.zeros((BLK, BLK), jnp.float32)
+        near = near_ref[t]
+        counted = jnp.zeros((BLK, BLK), jnp.bfloat16)
         for k in range(entries):
-            counted += jnp.where(places == near[k:k + 1, :], 1.0, 0.0)
-        return counted * softplus(dots * root)
+            counted += jnp.where(places == near[k:k + 1, :], one, none)
+        return counted.astype(jnp.float32) * softplus(dots * root)
 
     def mine(t):
         col = col_ref[t]
@@ -65,20 +68,37 @@
         emit(mat, slot, col_ref[t] - blocks, row_ref[t])
         count_ref[1] = slot - tiles + 1
 
-    @pl.loop(0, tiles)
-    def _(t):
-        mat = turned(t)
-        emit(mat.T, t, row_ref[t] - blocks, col_ref[t])
-
+    listed[0] = tiles
+
+    def note(t, found):
         @pl.when(mine(t))
         def _():
-            emit_back(t, mat)
-
-    @pl.loop(tiles, 3 * tiles)
-    def _(t):
-        @pl.when(mine(t))
-        def _():
-            emit_back(t, turned(t))
+            listed[found] = t
+
+        return found + mine(t).astype(jnp.int32)
+
+    found = lax.fori_loop(tiles, 3 * tiles, note, jnp.int32(0))
+
+    @pl.loop(0, tiles // GROUP)
+    def _(g):
+        ids = [g * GROUP + i for i in range(GROUP)]
+        mats = [turned(t) for t in ids]
+        for t, mat in zip(ids, mats):
+            emit(mat.T, t, row_ref[t] - blocks, col_ref[t])
+        for t, mat in zip(ids, mats):
+            @pl.when(mine(t))
+            def _(t=t, mat=mat):
+                emit_back(t, mat)
+
+    @pl.loop(0, pl.cdiv(found, GROUP))
+    def _(g):
+        at = [g * GROUP + i for i in range(GROUP)]
+        ids = [listed[jnp.minimum(n, found - 1)] for n in at]
+        mats = [turned(t) for t in ids]
+        for n, t, mat in zip(at, ids, mats):
+            @pl.when(n < found)
+            def _(t=t, mat=mat):
+                emit_back(t, mat)
 
     for place in range(STAGE):
         pltpu.make_async_copy(stage.at[place], mats_ref.at[0], sems.at[place]).wait()
@@ -103,6 +123,7 @@
         out_specs=(pl.BlockSpec(memory_space=pl.ANY), vmem, smem, smem, smem),
         scratch_shapes=[
             pltpu.VMEM((STAGE, BLK, 2 * BLK), jnp.bfloat16),
+            pltpu.SMEM((2 * tiles,), jnp.int32),
             pltpu.SemaphoreType.DMA((STAGE,)),
         ],
         compiler_params=pltpu.CompilerParams(vmem_limit_bytes=VMEM_LIMIT),
@@ -370,7 +391,7 @@
     )(*args)
 
 
-PIECES = 2
+PIECES = 4
 
 
 def gather_kernel(count, parts, own, near, window, near_all,
@@ -430,19 +451,16 @@
         ]
 
     order = [(piece, side) for piece in range(PIECES) for side in range(2)]
-    for piece, side in order:
-        @pl.when(sides[1 - side][0])
-        def _(piece=piece, side=side):
-            for copy in far[piece, side]:
-                copy.wait_recv()
-            for copy in forward(piece, side, 0):
-                copy.start()
-
-    for level in range(1, len(bits)):
-        for piece, side in order:
+    depth = len(bits)
+    for turn in range(len(order) + depth - 1):
+        for level in range(depth):
+            if not 0 <= turn - level < len(order):
+                continue
+            piece, side = order[turn - level]
+
             @pl.when(sides[1 - side][0])
             def _(piece=piece, side=side, level=level):
-                for copy in forward(piece, side, level - 1):
+                for copy in forward(piece, side, level - 1) if level else far[piece, side]:
                     copy.wait_recv()
                 for copy in forward(piece, side, level):
                     copy.start()

time: 315 us -> 317 us (level)
    pallas_call x4, Pallas kernels: 132 us -> 129 us  [swap(): pl.pallas_call(functools.partial(swap_kernel, count, field is not None, s...]
where the time goes in v3:
time: 317 us; the launch traced here: 316 us
  Pallas kernels  289 us (91%)
  other arithmetic  16.6 us (5%)
  matrix products  6.54 us (2%)
  local copies, waits for them, and re-layouts  3.24 us (1%)
    pallas_call x4, Pallas kernels, swap(): pl.pallas_call(functools.partial(swap_kernel, count, field is not None, s...  129 us
    pallas_call x1, Pallas kernels, gather(): pl.pallas_call(functools.partial(gather_kernel, count, parts), out_shape=...  76.7 us
    pallas_call x3, Pallas kernels, run_step(): pl.pallas_call(functools.partial(step_kernel, step, blocks, tiles), out_s...  44.1 us
    pallas_call x1, Pallas kernels, build(): pl.pallas_call(functools.partial(build_kernel, tiles, entries, blocks), o...  39.4 us
    dot_general x1, matrix products, per_device(): lax.dot_general(window, query_descriptors, (((1,), (1,)), ((), ())), pref...  6.54 us

profile of v3, /device:TPU:0, one launch (start us, length us, event | category | flops | bytes accessed | tf_op | source)
XLA Modules:
  0.0 316.3 jit_solution(3390123212019461598)
XLA Ops:
  0.6 0.0 copy-start
  0.7 0.1 pad_add_fusion
  0.7 0.8 subtract_convert_fusion
  1.5 0.7 compare_and_fusion
  2.1 0.1 broadcast_in_dim.18
  2.2 0.1 and.9
  2.3 0.7 broadcast_in_dim.17
  3.0 0.1 mul.75
  3.1 0.7 broadcast_in_dim.19
  3.8 0.1 mul.77
  3.9 0.1 copy.16
  4.0 1.0 convert.12
  5.1 0.1 copy.15
  5.2 0.8 fusion.2.near
  6.0 76.7 %gather_beside.1 = (bf16[6144,512]{1,0:T(8,128)(2,1)}, bf16[192,16,128]{2,1,0:T(8,128)(2,1)}) custom-call(bf16[2048,512]{1,0:T(8,128)(2,1)} %own.1, bf16[64,16,128]{2,1,0:T(8,128)(2,1)} %fusion.2.near), custom_call_target="tpu_custom_call" | custom-call | tf_op jit(solution)/shard_map/gather_beside/pallas_call | solution.py:492
  82.7 1.2 slice_convert_fusion
  83.9 0.2 slice_reduce_fusion.1
  84.1 0.5 add_select_fusion.col_ref
  84.7 0.6 add.42.row_ref
  85.2 0.0 copy-done
  85.2 6.5 %compare_select_fusion = f32[6144,128]{1,0:T(8,128)} fusion(bf16[6144,512]{1,0:T(8,128)(2,1)} %get-tuple-element.32.window_ref, bf16[128,512]{1,0:T(8,128)(2,1)S(1)} %copy-done), kind=kOutput, calls=%fused_computation | convolution fusion | flops 810811392 | bytes 9568256 | tf_op jit(solution)/shard_map/dot_general | solution.py:535
  91.8 39.4 %build_tiles.1 = (bf16[256,128,256]{2,1,0:T(8,128)(2,1)}, f32[2048,128]{1,0:T(8,128)}, s32[256]{0:T(256)}, s32[256]{0:T(256)}, s32[2]{0:T(128)}) custom-call(s32[192]{0:T(256)} %add.42.row_ref, s32[192]{0:T(256)} %add_select_fusion.col_ref, bf16[6144,512]{1,0:T(8,128)(2,1)} %get-tuple-element.32.window_ref, bf16[192,16,128]{2,1,0:T(8,128)(2,1)} %get-tuple-element.31.near_ref), custom_call_target="tpu_custom_call" | custom-call | tf_op jit(solution)/shard_map/build_tiles/pallas_call | solution.py:113
  131.2 1.4 add_rsqrt_fusion.refs_4_
  132.6 0.0 copy-start.1
  132.6 1.0 slice_reduce_fusion
  133.6 11.2 %swap.4 = (f32[16,128]{1,0:T(8,128)}, f32[16,128]{1,0:T(8,128)}) custom-call(f32[16,128]{1,0:T(8,128)} %bitcast.17), custom_call_target="tpu_custom_call" | custom-call | tf_op jit(solution)/shard_map/swap/pallas_call | solution.py:383
  144.8 3.0 slice_multiply_fusion.1
  147.7 0.0 copy-done.1
  147.7 1.4 pad_maximum_fusion.refs_6_.refs_9_
  149.2 12.8 %operator_step.3 = (f32[2048,128]{1,0:T(8,128)}, f32[8,128]{1,0:T(8,128)}, f32[2048,128]{1,0:T(8,128)}) custom-call(s32[256]{0:T(256)} %get-tuple-element.33.refs_0_, s32[256]{0:T(256)} %get-tuple-element.34.refs_1_, s32[2]{0:T(128)} %get-tuple-element.35.refs_2_, bf16[256,128,256]{2,1,0:T(8,128)(2,1)} %get-tuple-element.36.refs_3_, f32[2048,128]{1,0:T(8,128)} %copy-done.1, ...), custom_call_target="tpu_custom_call" | custom-call | tf_op jit(solution)/shard_map/operator_step/pallas_call | solution.py:269
  162.0 55.7 %swap.5 = (f32[2048,128]{1,0:T(8,128)}, f32[2048,128]{1,0:T(8,128)}, f32[8,128]{1,0:T(8,128)}) custom-call(f32[2048,128]{1,0:T(8,128)} %get-tuple-element.40.refs_0_, f32[8,128]{1,0:T(8,128)} %get-tuple-element.41.refs_1_), custom_call_target="tpu_custom_call" | custom-call | tf_op jit(solution)/shard_map/swap/pallas_call | solution.py:383
  217.7 16.2 %operator_step.4 = (f32[2048,128]{1,0:T(8,128)}, f32[2048,128]{1,0:T(8,128)}, f32[2048,128]{1,0:T(8,128)}, f32[8,128]{1,0:T(8,128)}, f32[2048,128]{1,0:T(8,128)}...) custom-call(s32[256]{0:T(256)} %get-tuple-element.33.refs_0_, s32[256]{0:T(256)} %get-tuple-element.34.refs_1_, ...), custom_call_target="tpu_custom_call" | custom-call | tf_op jit(solution)/shard_map/operator_step/pallas_call | solution.py:269
  233.9 51.0 %swap.6 = (f32[2048,128]{1,0:T(8,128)}, f32[2048,128]{1,0:T(8,128)}, f32[8,128]{1,0:T(8,128)}) custom-call(f32[2048,128]{1,0:T(8,128)} %get-tuple-element.46.refs_0_, f32[8,128]{1,0:T(8,128)} %get-tuple-element.47.refs_1_), custom_call_target="tpu_custom_call" | custom-call | tf_op jit(solution)/shard_map/swap/pallas_call | solution.py:383
  284.9 0.8 fusion.3
  285.7 0.0 copy-start.2
  285.7 15.1 %operator_step.5 = (f32[2048,128]{1,0:T(8,128)}, f32[2048,128]{1,0:T(8,128)}, f32[2048,128]{1,0:T(8,128)}, f32[8,128]{1,0:T(8,128)}) custom-call(s32[256]{0:T(256)} %get-tuple-element.33.refs_0_, s32[256]{0:T(256)} %get-tuple-element.34.refs_1_, s32[2]{0:T(128)} %get-tuple-element.35.refs_2_, bf16[256,128,256]{2,1,0:T(8,128)(2,1)} %get-tuple-element.36.refs_3_, ...), custom_call_target="tpu_custom_call" | custom-call | tf_op jit(solution)/shard_map/operator_step/pallas_call | solution.py:269
  300.8 11.0 %swap.7 = f32[8,128]{1,0:T(8,128)} custom-call(f32[8,128]{1,0:T(8,128)} %get-tuple-element.56.refs_0_), custom_call_target="tpu_custom_call" | custom-call | tf_op jit(solution)/shard_map/swap/pallas_call | solution.py:383
  311.8 0.8 fusion.5
  312.5 0.0 copy-done.2
  312.5 3.7 %multiply_subtract_fusion = (f32[2048,128]{1,0:T(8,128)}, f32[2048,128]{1,0:T(8,128)}) fusion(f32[2048,128]{1,0:T(8,128)} %get-tuple-element.58, f32[2048,128]{1,0:T(8,128)} %get-tuple-element.59, f32[128]{0:T(128)S(1)} %fusion.5, f32[2048,128]{1,0:T(8,128)} %get-tuple-element.57, f32[2048,128]{1,0:T(8,128)S(1)} %copy-done.2, f32[128]{0:T(128)S(1)} %get-tuple-element.68, ...), kind=kLoop, calls=%fused_computation.6 | loop fusion | flops 1835008 | bytes 7341568 | tf_op jit(solution)/shard_map/sub | solution.py:555
  (1 shorter events, 0.0 us)
Async XLA Ops:
  0.6 84.6 %copy-start = (bf16[128,512]{1,0:T(8,128)(2,1)S(1)}, bf16[128,512]{1,0:T(8,128)(2,1)}, u32[]{:S(2)}) copy-start(bf16[128,512]{1,0:T(8,128)(2,1)} %param.6) | copy-start | bytes 393220
  132.6 15.1 %copy-start.1 = (f32[2048,128]{1,0:T(8,128)}, f32[2048,128]{1,0:T(8,128)S(1)}, u32[]{:S(2)}) copy-start(f32[2048,128]{1,0:T(8,128)S(1)} %add_rsqrt_fusion.refs_4_) | copy-start | bytes 3145732
  285.7 26.8 %copy-start.2 = (f32[2048,128]{1,0:T(8,128)S(1)}, f32[2048,128]{1,0:T(8,128)}, u32[]{:S(2)}) copy-start(f32[2048,128]{1,0:T(8,128)} %get-tuple-element.49.refs_7_) | copy-start | bytes 3145732

commit v4 on v3

--- a/solution.py
+++ b/solution.py
@@ -20,8 +20,22 @@
     return jnp.maximum(value, 0.0) + jnp.log(1.0 + jnp.exp(-jnp.abs(value)))
 
 
-def build_kernel(tiles, entries, blocks, row_ref, col_ref, window_ref, near_ref,
-                 mats_ref, degree_ref, dst_ref, src_ref, count_ref, stage, listed, sems):
+def build_kernel(tiles, entries, blocks, row_ref, col_ref, own_ref, beside_ref, near_own, near_beside,
+                 mats_ref, degree_ref, dst_ref, src_ref, count_ref,
+                 window_ref, near_ref, stage, listed, load_sems, sems):
+    size = blocks * BLK
+    loads = [
+        pltpu.make_async_copy(src, dst, load_sems.at[i])
+        for i, (src, dst) in enumerate((
+            (own_ref, window_ref.at[pl.ds(size, size)]),
+            (beside_ref.at[pl.ds(0, size)], window_ref.at[pl.ds(0, size)]),
+            (beside_ref.at[pl.ds(size, size)], window_ref.at[pl.ds(2 * size, size)]),
+            (near_own, near_ref.at[pl.ds(0, tiles)]),
+            (near_beside, near_ref.at[pl.ds(tiles, 2 * tiles)]),
+        ))
+    ]
+    for load in loads:
+        load.start()
     root = 1.0 / math.sqrt(window_ref.shape[1])
     degree_ref[...] = jnp.zeros_like(degree_ref)
     count_ref[0] = 0
@@ -78,6 +92,8 @@
         return found + mine(t).astype(jnp.int32)
 
     found = lax.fori_loop(tiles, 3 * tiles, note, jnp.int32(0))
+    for load in loads:
+        load.wait()
 
     @pl.loop(0, tiles // GROUP)
     def _(g):
@@ -104,10 +120,10 @@
         pltpu.make_async_copy(stage.at[place], mats_ref.at[0], sems.at[place]).wait()
 
 
-def build(entries, row, col, window, near):
-    total = near.shape[0]
-    tiles = total // 3
-    blocks = window.shape[0] // (3 * BLK)
+def build(entries, row, col, own, beside, near, near_beside):
+    tiles = near.shape[0]
+    blocks = own.shape[0] // BLK
+    anywhere = pl.BlockSpec(memory_space=pl.ANY)
     smem = pl.BlockSpec(memory_space=pltpu.SMEM)
     vmem = pl.BlockSpec(memory_space=pltpu.VMEM)
     return pl.pallas_call(
@@ -119,16 +135,19 @@
             jax.ShapeDtypeStruct((4 * tiles,), jnp.int32),
             jax.ShapeDtypeStruct((2,), jnp.int32),
         ),
-        in_specs=[smem, smem, vmem, vmem],
+        in_specs=[smem, smem] + [anywhere] * 4,
         out_specs=(pl.BlockSpec(memory_space=pl.ANY), vmem, smem, smem, smem),
         scratch_shapes=[
+            pltpu.VMEM((3 * own.shape[0],) + own.shape[1:], own.dtype),
+            pltpu.VMEM((3 * tiles,) + near.shape[1:], near.dtype),
             pltpu.VMEM((STAGE, BLK, 2 * BLK), jnp.bfloat16),
             pltpu.SMEM((2 * tiles,), jnp.int32),
+            pltpu.SemaphoreType.DMA((5,)),
             pltpu.SemaphoreType.DMA((STAGE,)),
         ],
         compiler_params=pltpu.CompilerParams(vmem_limit_bytes=VMEM_LIMIT),
         name="build_tiles",
-    )(row, col, window, near)
+    )(row, col, own, beside, near, near_beside)
 
 
 def step_kernel(step, blocks, tiles, *refs):
@@ -391,11 +410,12 @@
     )(*args)
 
 
-PIECES = 4
+PIECES = 8
+FLIGHT = 3
 
 
 def gather_kernel(count, parts, own, near, window, near_all,
-                  far_send, far_recv, local_sems, *level_sems):
+                  far_send, far_recv, *level_sems):
     rows, tiles = own.shape[0], near.shape[0]
     size, tile_size = rows // parts, tiles // parts
     step, tile_step = size // PIECES, tile_size // PIECES
@@ -408,16 +428,12 @@
 
     signal_all([(exists, "gal", index) for exists, index in sides]
                + [(None, "qry", partner(bit)) for bit in bits])
-    locals_ = [
-        pltpu.make_async_copy(own, window.at[pl.ds(rows, rows)], local_sems.at[0]),
-        pltpu.make_async_copy(near, near_all.at[pl.ds(0, tiles)], local_sems.at[1]),
-    ]
 
     def pair(index, piece, side):
         at = index * size + piece * step
         near_at = index * tile_size + piece * tile_step
-        base = (0, 2 * rows)[side]
-        near_base = (tiles, 2 * tiles)[side]
+        base = (0, rows)[side]
+        near_base = (0, tiles)[side]
         return (
             (own.at[pl.ds(at, step)], window.at[pl.ds(base + at, step)]),
             (near.at[pl.ds(near_at, tile_step)], near_all.at[pl.ds(near_base + near_at, tile_step)]),
@@ -430,12 +446,15 @@
                 remote(src, dst, far_send.at[piece, i, k], far_recv.at[piece, i, k], "gal", index)
                 for k, (src, dst) in enumerate(pair(part, piece, i))
             ]
-    for piece in range(PIECES):
-        for i, (exists, _) in enumerate(sides):
-            for copy in far[piece, i]:
-                pl.when(exists)(copy.start)
-    for copy in locals_:
-        copy.start()
+    def launch(piece, side):
+        @pl.when(sides[side][0])
+        def _():
+            for copy in far[piece, side]:
+                copy.start()
+
+    for piece in range(FLIGHT):
+        for side in range(2):
+            launch(piece, side)
 
     def forward(piece, side, level):
         bit = bits[level]
@@ -465,6 +484,15 @@
                 for copy in forward(piece, side, level):
                     copy.start()
 
+            if level == 0:
+                @pl.when(sides[side][0])
+                def _(piece=piece, side=side):
+                    for copy in far[piece, side]:
+                        copy.wait_send()
+
+                if piece + FLIGHT < PIECES:
+                    launch(piece + FLIGHT, side)
+
     for piece, side in order:
         @pl.when(sides[1 - side][0])
         def _(piece=piece, side=side):
@@ -473,14 +501,6 @@
             for level in range(len(bits)):
                 for copy in forward(piece, side, level):
                     copy.wait_send()
-
-        @pl.when(sides[side][0])
-        def _(piece=piece, side=side):
-            for copy in far[piece, side]:
-                copy.wait_send()
-
-    for copy in locals_:
-        copy.wait()
 
 
 def gather(own, near):
@@ -492,15 +512,14 @@
     return pl.pallas_call(
         functools.partial(gather_kernel, count, parts),
         out_shape=(
-            jax.ShapeDtypeStruct((3 * own.shape[0],) + own.shape[1:], own.dtype),
-            jax.ShapeDtypeStruct((3 * near.shape[0],) + near.shape[1:], near.dtype),
+            jax.ShapeDtypeStruct((2 * own.shape[0],) + own.shape[1:], own.dtype),
+            jax.ShapeDtypeStruct((2 * near.shape[0],) + near.shape[1:], near.dtype),
         ),
         in_specs=[anywhere] * 2,
         out_specs=(anywhere, anywhere),
         scratch_shapes=[
             pltpu.SemaphoreType.DMA((PIECES, 2, 2)),
             pltpu.SemaphoreType.DMA((PIECES, 2, 2)),
-            pltpu.SemaphoreType.DMA((2,)),
         ] + levels,
         compiler_params=pltpu.CompilerParams(collective_id=0, has_side_effects=True),
         name="gather_beside",
@@ -520,26 +539,27 @@
     spots = jnp.pad(spot, ((0, 0), (0, BLK - 2)))[:, None, :]
     near = jnp.concatenate([neighbours, spots], axis=1)
     near = jnp.pad(near, ((0, 0), (0, 16 - entries - 1), (0, 0))).astype(jnp.bfloat16)
-    window, near_all = gather(descriptors, near)
-    spots = near_all[:, entries, 0:2].astype(jnp.int32)
-    shift = jnp.repeat(jnp.array([0, -1, 1], jnp.int32), tiles)
+    beside, near_beside = gather(descriptors, near)
+    spots = near_beside[:, entries, 0:2].astype(jnp.int32)
+    shift = jnp.repeat(jnp.array([-1, 1], jnp.int32), tiles)
     origin = shift + place
     exists = jnp.logical_and(origin >= 0, origin < count)
-    row = spots[:, 0] + (1 + shift) * blocks
-    col = jnp.where(exists, spots[:, 1] + shift * blocks, jnp.int32(3 * blocks))
-
-    mats, degree, dst, src, used = build(entries, row, col, window, near_all)
+    row = jnp.concatenate([spot[:, 0] + blocks, spots[:, 0] + (1 + shift) * blocks])
+    col = jnp.concatenate(
+        [spot[:, 1], jnp.where(exists, spots[:, 1] + shift * blocks, jnp.int32(3 * blocks))]
+    )
+
+    mats, degree, dst, src, used = build(entries, row, col, descriptors, beside, near, near_beside)
     scale = 1.0 / jnp.sqrt(1.0 + degree)
     scale_low, scale_high = swap(1, scale[:, 0].reshape(blocks, BLK))
-    seeds = jax.nn.softplus(
-        lax.dot_general(window, query_descriptors, (((1,), (1,)), ((), ())),
-                        preferred_element_type=jnp.float32) / math.sqrt(width)
-    )
-    own = seeds[rows:2 * rows]
-    halo = jnp.concatenate(
-        [seeds[:rows] * scale_low.reshape(rows, 1), seeds[2 * rows:] * scale_high.reshape(rows, 1)],
-        axis=0,
-    )
+
+    def seeds(field):
+        dots = lax.dot_general(field, query_descriptors, (((1,), (1,)), ((), ())),
+                               preferred_element_type=jnp.float32)
+        return jax.nn.softplus(dots / math.sqrt(width))
+
+    own = seeds(descriptors)
+    halo = seeds(beside) * jnp.concatenate([scale_low, scale_high]).reshape(2 * rows, 1)
     image0, sums0, send0 = run_step(0, dst, src, used, mats, scale, own, halo)
     low0, high0, sums0 = swap(2, send0, sums0)
     res1, dir1, image1, sums1, send1, halo1, tail1 = run_step(

time: 317 us -> 281 us (0.89)
  Pallas kernels: 289 us -> 256 us
  other arithmetic: 16.6 us -> 11.7 us
    pallas_call x1, Pallas kernels: 76.7 us -> 44.2 us  [gather(): pl.pallas_call(functools.partial(gather_kernel, count, parts), out_shape=...]
    dot_general x1 -> x2, matrix products: 6.54 us -> 7.03 us  [seeds(): lax.dot_general(field, query_descriptors, (((1,), (1,)), ((), ())), prefe...]
where the time goes in v4:
time: 281 us; the launch traced here: 278 us
  Pallas kernels  256 us (91%)
  other arithmetic  11.7 us (4%)
  matrix products  7.03 us (3%)
    pallas_call x4, Pallas kernels, swap(): pl.pallas_call(functools.partial(swap_kernel, count, field is not None, s...  128 us
    pallas_call x3, Pallas kernels, run_step(): pl.pallas_call(functools.partial(step_kernel, step, blocks, tiles), out_s...  44.9 us
    pallas_call x1, Pallas kernels, gather(): pl.pallas_call(functools.partial(gather_kernel, count, parts), out_shape=...  44.2 us
    pallas_call x1, Pallas kernels, build(): pl.pallas_call(functools.partial(build_kernel, tiles, entries, blocks), o...  39.2 us
    dot_general x2, matrix products, seeds(): lax.dot_general(field, query_descriptors, (((1,), (1,)), ((), ())), prefe...  7.03 us

profile of v4, /device:TPU:0, one launch (start us, length us, event | category | flops | bytes accessed | tf_op | source)
XLA Modules:
  0.0 278.1 jit_solution(6321322728613087210)
XLA Ops:
  0.6 0.0 copy-start
  0.7 0.1 pad_add_fusion.2
  0.7 0.8 copy.12
  1.6 0.0 copy-start.6
  1.6 0.0 copy-start.5
  1.6 1.0 convert.12
  2.6 0.1 copy.13
  2.8 0.8 fusion.3.near.near_own
  3.6 44.2 %gather_beside.1 = (bf16[4096,512]{1,0:T(8,128)(2,1)}, bf16[128,16,128]{2,1,0:T(8,128)(2,1)}) custom-call(bf16[2048,512]{1,0:T(8,128)(2,1)} %own_ref.1, bf16[64,16,128]{2,1,0:T(8,128)(2,1)} %fusion.3.near.near_own), custom_call_target="tpu_custom_call" | custom-call | tf_op jit(solution)/shard_map/gather_beside/pallas_call | solution.py:512
  47.8 1.1 slice_convert_fusion
  48.9 0.2 slice_reduce_fusion.1
  49.1 0.0 copy-done.6
  49.1 0.1 broadcast_in_dim.18
  49.2 0.1 and.9
  49.2 0.0 copy-done.5
  49.2 0.1 broadcast_in_dim.19
  49.3 0.1 mul.67
  49.4 0.1 broadcast_in_dim.17
  49.5 0.1 mul.65
  49.6 0.2 slice_reduce_fusion.3
  49.8 0.7 pad_add_fusion
  50.4 39.2 %build_tiles.1 = (bf16[256,128,256]{2,1,0:T(8,128)(2,1)}, f32[2048,128]{1,0:T(8,128)}, s32[256]{0:T(256)}, s32[256]{0:T(256)}, s32[2]{0:T(128)}) custom-call(s32[192]{0:T(256)} %get-tuple-element.68.row_ref, s32[192]{0:T(256)} %get-tuple-element.69.col_ref, bf16[2048,512]{1,0:T(8,128)(2,1)} %own_ref.1, bf16[4096,512]{1,0:T(8,128)(2,1)} %get-tuple-element.32.beside_ref, ...), custom_call_target="tpu_custom_call" | custom-call | tf_op jit(solution)/shard_map/build_tiles/pallas_call | solution.py:129
  89.6 1.4 add_rsqrt_fusion.refs_4_
  91.0 0.0 copy-start.1
  91.0 1.0 slice_reduce_fusion
  92.0 14.1 %swap.4 = (f32[16,128]{1,0:T(8,128)}, f32[16,128]{1,0:T(8,128)}) custom-call(f32[16,128]{1,0:T(8,128)} %bitcast.19), custom_call_target="tpu_custom_call" | custom-call | tf_op jit(solution)/shard_map/swap/pallas_call | solution.py:402
  106.1 0.7 maximum_bitcast_fusion
  106.8 0.0 copy-done
  106.8 0.0 copy-start.3
  106.8 5.2 %fusion.refs_6_.refs_9_ = f32[4096,128]{1,0:T(8,128)} fusion(bf16[4096,512]{1,0:T(8,128)(2,1)} %get-tuple-element.32.beside_ref, bf16[128,512]{1,0:T(8,128)(2,1)S(1)} %copy-done, f32[4096]{0:T(1024)S(1)} %maximum_bitcast_fusion), kind=kOutput, calls=%fused_computation.4 | convolution fusion | flops 541065216 | bytes 6438912 | tf_op jit(solution)/shard_map/dot_general | solution.py:557
  112.1 0.0 copy-done.1
  112.1 0.0 copy-done.3
  112.1 1.8 compare_select_fusion.1.refs_5_.refs_6_.refs_7_
  113.8 13.1 %operator_step.3 = (f32[2048,128]{1,0:T(8,128)}, f32[8,128]{1,0:T(8,128)}, f32[2048,128]{1,0:T(8,128)}) custom-call(s32[256]{0:T(256)} %get-tuple-element.33.refs_0_, s32[256]{0:T(256)} %get-tuple-element.34.refs_1_, s32[2]{0:T(128)} %get-tuple-element.35.refs_2_, bf16[256,128,256]{2,1,0:T(8,128)(2,1)} %get-tuple-element.36.refs_3_, f32[2048,128]{1,0:T(8,128)} %copy-done.1, ...), custom_call_target="tpu_custom_call" | custom-call | tf_op jit(solution)/shard_map/operator_step/pallas_call | solution.py:288
  126.9 53.4 %swap.5 = (f32[2048,128]{1,0:T(8,128)}, f32[2048,128]{1,0:T(8,128)}, f32[8,128]{1,0:T(8,128)}) custom-call(f32[2048,128]{1,0:T(8,128)} %get-tuple-element.40.refs_0_, f32[8,128]{1,0:T(8,128)} %get-tuple-element.41.refs_1_), custom_call_target="tpu_custom_call" | custom-call | tf_op jit(solution)/shard_map/swap/pallas_call | solution.py:402
  180.3 16.5 %operator_step.4 = (f32[2048,128]{1,0:T(8,128)}, f32[2048,128]{1,0:T(8,128)}, f32[2048,128]{1,0:T(8,128)}, f32[8,128]{1,0:T(8,128)}, f32[2048,128]{1,0:T(8,128)}...) custom-call(s32[256]{0:T(256)} %get-tuple-element.33.refs_0_, s32[256]{0:T(256)} %get-tuple-element.34.refs_1_, ...), custom_call_target="tpu_custom_call" | custom-call | tf_op jit(solution)/shard_map/operator_step/pallas_call | solution.py:288
  196.8 50.4 %swap.6 = (f32[2048,128]{1,0:T(8,128)}, f32[2048,128]{1,0:T(8,128)}, f32[8,128]{1,0:T(8,128)}) custom-call(f32[2048,128]{1,0:T(8,128)} %get-tuple-element.46.refs_0_, f32[8,128]{1,0:T(8,128)} %get-tuple-element.47.refs_1_), custom_call_target="tpu_custom_call" | custom-call | tf_op jit(solution)/shard_map/swap/pallas_call | solution.py:402
  247.2 0.0 copy-start.2
  247.2 0.0 copy-start.4
  247.2 15.4 %operator_step.5 = (f32[2048,128]{1,0:T(8,128)}, f32[2048,128]{1,0:T(8,128)}, f32[2048,128]{1,0:T(8,128)}, f32[8,128]{1,0:T(8,128)}) custom-call(s32[256]{0:T(256)} %get-tuple-element.33.refs_0_, s32[256]{0:T(256)} %get-tuple-element.34.refs_1_, s32[2]{0:T(128)} %get-tuple-element.35.refs_2_, bf16[256,128,256]{2,1,0:T(8,128)(2,1)} %get-tuple-element.36.refs_3_, ...), custom_call_target="tpu_custom_call" | custom-call | tf_op jit(solution)/shard_map/operator_step/pallas_call | solution.py:288
  262.6 9.8 %swap.7 = f32[8,128]{1,0:T(8,128)} custom-call(f32[8,128]{1,0:T(8,128)} %get-tuple-element.56.refs_0_), custom_call_target="tpu_custom_call" | custom-call | tf_op jit(solution)/shard_map/swap/pallas_call | solution.py:402
  272.3 0.8 fusion.7
  273.1 0.8 fusion.6
  273.9 0.8 fusion.5
  274.6 0.0 copy-done.2
  274.6 0.0 copy-done.4
  274.6 3.4 %multiply_subtract_fusion = (f32[2048,128]{1,0:T(8,128)}, f32[2048,128]{1,0:T(8,128)}) fusion(f32[2048,128]{1,0:T(8,128)} %get-tuple-element.58, f32[2048,128]{1,0:T(8,128)} %get-tuple-element.59, f32[128]{0:T(128)S(1)} %fusion.7, f32[2048,128]{1,0:T(8,128)} %get-tuple-element.57, f32[2048,128]{1,0:T(8,128)S(1)} %copy-done.4, f32[128]{0:T(128)S(1)} %fusion.6, ...), kind=kLoop, calls=%fused_computation.6 | loop fusion | flops 1835008 | bytes 7341568 | tf_op jit(solution)/shard_map/sub | solution.py:575
  (7 shorter events, 0.1 us)
Async XLA Ops:
  0.6 106.2 %copy-start = (bf16[128,512]{1,0:T(8,128)(2,1)S(1)}, bf16[128,512]{1,0:T(8,128)(2,1)}, u32[]{:S(2)}) copy-start(bf16[128,512]{1,0:T(8,128)(2,1)} %param.6) | copy-start | bytes 393220
  1.6 47.5 %copy-start.6 = (s32[2]{0:T(128)S(1)}, s32[2]{0:T(128)}, u32[]{:S(2)}) copy-start(s32[2]{0:T(128)} %constant.37.clone) | copy-start | bytes 28
  1.6 47.7 %copy-start.5 = (s32[2]{0:T(128)S(1)}, s32[2]{0:T(128)}, u32[]{:S(2)}) copy-start(s32[2]{0:T(128)} %constant.44) | copy-start | bytes 28
  91.0 21.1 %copy-start.1 = (f32[2048,128]{1,0:T(8,128)}, f32[2048,128]{1,0:T(8,128)S(1)}, u32[]{:S(2)}) copy-start(f32[2048,128]{1,0:T(8,128)S(1)} %add_rsqrt_fusion.refs_4_) | copy-start | bytes 3145732
  106.8 5.3 %copy-start.3 = (bf16[2048,512]{1,0:T(8,128)(2,1)S(1)}, bf16[2048,512]{1,0:T(8,128)(2,1)}, u32[]{:S(2)}) copy-start(bf16[2048,512]{1,0:T(8,128)(2,1)} %own_ref.1) | copy-start | bytes 6291460
  247.2 27.5 %copy-start.2 = (f32[2048,128]{1,0:T(8,128)S(1)}, f32[2048,128]{1,0:T(8,128)}, u32[]{:S(2)}) copy-start(f32[2048,128]{1,0:T(8,128)} %compare_select_fusion.1.refs_5_.refs_6_.refs_7_) | copy-start | bytes 3145732
  247.2 27.5 %copy-start.4 = (f32[2048,128]{1,0:T(8,128)S(1)}, f32[2048,128]{1,0:T(8,128)}, u32[]{:S(2)}) copy-start(f32[2048,128]{1,0:T(8,128)} %get-tuple-element.49.refs_7_) | copy-start | bytes 3145732

commit v5 on v4

--- a/solution.py
+++ b/solution.py
@@ -11,7 +11,8 @@
 BLK = 128
 DAMPING = 0.99
 STAGE = 8
-GROUP = 2
+GROUP = 4
+SHARES = 4
 CHUNK = 16
 VMEM_LIMIT = 60 * 1024 * 1024
 
@@ -358,12 +359,16 @@
             copy.start()
     if with_field:
         send, recv = refs
-        copies = [
-            remote(field, outs[i], send.at[i], recv.at[i], "gal", index)
+        shares = send.shape[1]
+        length = field.shape[0] // shares
+        copies = {
+            (i, n): remote(field.at[pl.ds(n * length, length)], outs[i].at[pl.ds(n * length, length)],
+                           send.at[i, n], recv.at[i, n], "gal", index)
+            for n in range(shares)
             for i, (_, index) in enumerate(sides)
-        ]
-        for copy, (exists, _) in zip(copies, sides):
-            pl.when(exists)(copy.start)
+        }
+        for (i, _), copy in copies.items():
+            pl.when(sides[i][0])(copy.start)
     if with_sums:
         for copy in sends:
             copy.wait()
@@ -372,9 +377,9 @@
             all_sums += slots[o]
         sums_out[...] = all_sums
     if with_field:
-        for i in range(2):
-            pl.when(sides[i][0])(copies[i].wait_send)
-            pl.when(sides[1 - i][0])(copies[i].wait_recv)
+        for (i, _), copy in copies.items():
+            pl.when(sides[i][0])(copy.wait_send)
+            pl.when(sides[1 - i][0])(copy.wait_recv)
 
 
 def swap(ident, field=None, sums=None):
@@ -398,7 +403,8 @@
             pltpu.SemaphoreType.DMA((count,)),
         ]
     if field is not None:
-        scratch += [pltpu.SemaphoreType.DMA((2,)), pltpu.SemaphoreType.DMA((2,))]
+        shares = SHARES if field.shape[0] % (SHARES * BLK) == 0 else 1
+        scratch += [pltpu.SemaphoreType.DMA((2, shares)), pltpu.SemaphoreType.DMA((2, shares))]
     return pl.pallas_call(
         functools.partial(swap_kernel, count, field is not None, sums is not None),
         out_shape=tuple(outs),

time: 281 us -> 273 us (0.972)
  Pallas kernels: 256 us -> 250 us
    pallas_call x1, Pallas kernels: 39.2 us -> 33.7 us  [build(): pl.pallas_call(functools.partial(build_kernel, tiles, entries, blocks), o...]
where the time goes in v5:
time: 273 us; the launch traced here: 272 us
  Pallas kernels  250 us (92%)
  other arithmetic  11.7 us (4%)
  matrix products  7.03 us (3%)
    pallas_call x4, Pallas kernels, swap(): pl.pallas_call(functools.partial(swap_kernel, count, field is not None, s...  127 us
    pallas_call x3, Pallas kernels, run_step(): pl.pallas_call(functools.partial(step_kernel, step, blocks, tiles), out_s...  45.2 us
    pallas_call x1, Pallas kernels, gather(): pl.pallas_call(functools.partial(gather_kernel, count, parts), out_shape=...  44.2 us
    pallas_call x1, Pallas kernels, build(): pl.pallas_call(functools.partial(build_kernel, tiles, entries, blocks), o...  33.7 us
    dot_general x2, matrix products, seeds(): lax.dot_general(field, query_descriptors, (((1,), (1,)), ((), ())), prefe...  7.03 us

profile of v5, /device:TPU:0, one launch (start us, length us, event | category | flops | bytes accessed | tf_op | source)
XLA Modules:
  0.0 272.2 jit_solution(14045533978319464121)
XLA Ops:
  0.6 0.0 copy-start
  0.7 0.1 pad_add_fusion.2
  0.7 0.8 copy.12
  1.6 0.0 copy-start.6
  1.6 0.0 copy-start.5
  1.6 1.0 convert.12
  2.6 0.1 copy.13
  2.8 0.8 fusion.3.near.near_own
  3.6 44.2 %gather_beside.1 = (bf16[4096,512]{1,0:T(8,128)(2,1)}, bf16[128,16,128]{2,1,0:T(8,128)(2,1)}) custom-call(bf16[2048,512]{1,0:T(8,128)(2,1)} %own_ref.1, bf16[64,16,128]{2,1,0:T(8,128)(2,1)} %fusion.3.near.near_own), custom_call_target="tpu_custom_call" | custom-call | tf_op jit(solution)/shard_map/gather_beside/pallas_call | solution.py:518
  47.8 1.1 slice_convert_fusion
  48.9 0.2 slice_reduce_fusion.1
  49.1 0.0 copy-done.6
  49.1 0.1 broadcast_in_dim.18
  49.2 0.1 and.9
  49.2 0.0 copy-done.5
  49.2 0.1 broadcast_in_dim.19
  49.3 0.1 mul.67
  49.4 0.1 broadcast_in_dim.17
  49.5 0.1 mul.65
  49.6 0.2 slice_reduce_fusion.3
  49.8 0.7 pad_add_fusion
  50.4 33.7 %build_tiles.1 = (bf16[256,128,256]{2,1,0:T(8,128)(2,1)}, f32[2048,128]{1,0:T(8,128)}, s32[256]{0:T(256)}, s32[256]{0:T(256)}, s32[2]{0:T(128)}) custom-call(s32[192]{0:T(256)} %get-tuple-element.68.row_ref, s32[192]{0:T(256)} %get-tuple-element.69.col_ref, bf16[2048,512]{1,0:T(8,128)(2,1)} %own_ref.1, bf16[4096,512]{1,0:T(8,128)(2,1)} %get-tuple-element.32.beside_ref, ...), custom_call_target="tpu_custom_call" | custom-call | tf_op jit(solution)/shard_map/build_tiles/pallas_call | solution.py:130
  84.2 1.4 add_rsqrt_fusion.refs_4_
  85.5 0.0 copy-start.1
  85.6 1.0 slice_reduce_fusion
  86.5 13.8 %swap.4 = (f32[16,128]{1,0:T(8,128)}, f32[16,128]{1,0:T(8,128)}) custom-call(f32[16,128]{1,0:T(8,128)} %bitcast.19), custom_call_target="tpu_custom_call" | custom-call | tf_op jit(solution)/shard_map/swap/pallas_call | solution.py:408
  100.4 0.7 maximum_bitcast_fusion
  101.1 0.0 copy-done
  101.1 0.0 copy-start.3
  101.1 5.2 %fusion.refs_6_.refs_9_ = f32[4096,128]{1,0:T(8,128)} fusion(bf16[4096,512]{1,0:T(8,128)(2,1)} %get-tuple-element.32.beside_ref, bf16[128,512]{1,0:T(8,128)(2,1)S(1)} %copy-done, f32[4096]{0:T(1024)S(1)} %maximum_bitcast_fusion), kind=kOutput, calls=%fused_computation.4 | convolution fusion | flops 541065216 | bytes 6438912 | tf_op jit(solution)/shard_map/dot_general | solution.py:563
  106.3 0.0 copy-done.1
  106.3 0.0 copy-done.3
  106.3 1.8 compare_select_fusion.1.refs_5_.refs_6_.refs_7_
  108.1 13.2 %operator_step.3 = (f32[2048,128]{1,0:T(8,128)}, f32[8,128]{1,0:T(8,128)}, f32[2048,128]{1,0:T(8,128)}) custom-call(s32[256]{0:T(256)} %get-tuple-element.33.refs_0_, s32[256]{0:T(256)} %get-tuple-element.34.refs_1_, s32[2]{0:T(128)} %get-tuple-element.35.refs_2_, bf16[256,128,256]{2,1,0:T(8,128)(2,1)} %get-tuple-element.36.refs_3_, f32[2048,128]{1,0:T(8,128)} %copy-done.1, ...), custom_call_target="tpu_custom_call" | custom-call | tf_op jit(solution)/shard_map/operator_step/pallas_call | solution.py:289
  121.3 51.5 %swap.5 = (f32[2048,128]{1,0:T(8,128)}, f32[2048,128]{1,0:T(8,128)}, f32[8,128]{1,0:T(8,128)}) custom-call(f32[2048,128]{1,0:T(8,128)} %get-tuple-element.40.refs_0_, f32[8,128]{1,0:T(8,128)} %get-tuple-element.41.refs_1_), custom_call_target="tpu_custom_call" | custom-call | tf_op jit(solution)/shard_map/swap/pallas_call | solution.py:408
  172.8 16.6 %operator_step.4 = (f32[2048,128]{1,0:T(8,128)}, f32[2048,128]{1,0:T(8,128)}, f32[2048,128]{1,0:T(8,128)}, f32[8,128]{1,0:T(8,128)}, f32[2048,128]{1,0:T(8,128)}...) custom-call(s32[256]{0:T(256)} %get-tuple-element.33.refs_0_, s32[256]{0:T(256)} %get-tuple-element.34.refs_1_, ...), custom_call_target="tpu_custom_call" | custom-call | tf_op jit(solution)/shard_map/operator_step/pallas_call | solution.py:289
  189.4 51.6 %swap.6 = (f32[2048,128]{1,0:T(8,128)}, f32[2048,128]{1,0:T(8,128)}, f32[8,128]{1,0:T(8,128)}) custom-call(f32[2048,128]{1,0:T(8,128)} %get-tuple-element.46.refs_0_, f32[8,128]{1,0:T(8,128)} %get-tuple-element.47.refs_1_), custom_call_target="tpu_custom_call" | custom-call | tf_op jit(solution)/shard_map/swap/pallas_call | solution.py:408
  241.0 0.0 copy-start.2
  241.0 0.0 copy-start.4
  241.0 15.5 %operator_step.5 = (f32[2048,128]{1,0:T(8,128)}, f32[2048,128]{1,0:T(8,128)}, f32[2048,128]{1,0:T(8,128)}, f32[8,128]{1,0:T(8,128)}) custom-call(s32[256]{0:T(256)} %get-tuple-element.33.refs_0_, s32[256]{0:T(256)} %get-tuple-element.34.refs_1_, s32[2]{0:T(128)} %get-tuple-element.35.refs_2_, bf16[256,128,256]{2,1,0:T(8,128)(2,1)} %get-tuple-element.36.refs_3_, ...), custom_call_target="tpu_custom_call" | custom-call | tf_op jit(solution)/shard_map/operator_step/pallas_call | solution.py:289
  256.5 10.0 %swap.7 = f32[8,128]{1,0:T(8,128)} custom-call(f32[8,128]{1,0:T(8,128)} %get-tuple-element.56.refs_0_), custom_call_target="tpu_custom_call" | custom-call | tf_op jit(solution)/shard_map/swap/pallas_call | solution.py:408
  266.4 0.8 fusion.7
  267.2 0.8 fusion.6
  268.0 0.8 fusion.5
  268.7 0.0 copy-done.2
  268.7 0.0 copy-done.4
  268.7 3.4 %multiply_subtract_fusion = (f32[2048,128]{1,0:T(8,128)}, f32[2048,128]{1,0:T(8,128)}) fusion(f32[2048,128]{1,0:T(8,128)} %get-tuple-element.58, f32[2048,128]{1,0:T(8,128)} %get-tuple-element.59, f32[128]{0:T(128)S(1)} %fusion.7, f32[2048,128]{1,0:T(8,128)} %get-tuple-element.57, f32[2048,128]{1,0:T(8,128)S(1)} %copy-done.4, f32[128]{0:T(128)S(1)} %fusion.6, ...), kind=kLoop, calls=%fused_computation.6 | loop fusion | flops 1835008 | bytes 7341568 | tf_op jit(solution)/shard_map/sub | solution.py:581
  (7 shorter events, 0.1 us)
Async XLA Ops:
  0.6 100.5 %copy-start = (bf16[128,512]{1,0:T(8,128)(2,1)S(1)}, bf16[128,512]{1,0:T(8,128)(2,1)}, u32[]{:S(2)}) copy-start(bf16[128,512]{1,0:T(8,128)(2,1)} %param.6) | copy-start | bytes 393220
  1.6 47.5 %copy-start.6 = (s32[2]{0:T(128)S(1)}, s32[2]{0:T(128)}, u32[]{:S(2)}) copy-start(s32[2]{0:T(128)} %constant.37.clone) | copy-start | bytes 28
  1.6 47.7 %copy-start.5 = (s32[2]{0:T(128)S(1)}, s32[2]{0:T(128)}, u32[]{:S(2)}) copy-start(s32[2]{0:T(128)} %constant.44) | copy-start | bytes 28
  85.5 20.8 %copy-start.1 = (f32[2048,128]{1,0:T(8,128)}, f32[2048,128]{1,0:T(8,128)S(1)}, u32[]{:S(2)}) copy-start(f32[2048,128]{1,0:T(8,128)S(1)} %add_rsqrt_fusion.refs_4_) | copy-start | bytes 3145732
  101.1 5.3 %copy-start.3 = (bf16[2048,512]{1,0:T(8,128)(2,1)S(1)}, bf16[2048,512]{1,0:T(8,128)(2,1)}, u32[]{:S(2)}) copy-start(bf16[2048,512]{1,0:T(8,128)(2,1)} %own_ref.1) | copy-start | bytes 6291460
  241.0 27.8 %copy-start.2 = (f32[2048,128]{1,0:T(8,128)S(1)}, f32[2048,128]{1,0:T(8,128)}, u32[]{:S(2)}) copy-start(f32[2048,128]{1,0:T(8,128)} %compare_select_fusion.1.refs_5_.refs_6_.refs_7_) | copy-start | bytes 3145732
  241.0 27.8 %copy-start.4 = (f32[2048,128]{1,0:T(8,128)S(1)}, f32[2048,128]{1,0:T(8,128)}, u32[]{:S(2)}) copy-start(f32[2048,128]{1,0:T(8,128)} %get-tuple-element.49.refs_7_) | copy-start | bytes 3145732
